TPU v7x, 128 devices: a whole 4x4x4 slice. The times are simulated.
128 devices in a mesh: fs: 4 (over y), cp: 4 (over z), ul: 8 (over x, core).
Axes of the slice: x: 4, y: 4, z: 4, core: 2. Of those that a mesh axis runs over, the one named last changes fastest.
Arguments:
- tokens: bfloat16 [16384, 1024], P(('fs', 'cp', 'ul')), may hold values from -6 to 6
- norm_in: float32 [1024], replicated, may hold values from 0.5 to 1.5
- norm_mid: float32 [1024], replicated, may hold values from 0.5 to 1.5
- mamba_gain: float32 [1536], replicated, may hold values from 0.5 to 1.5
- conv_weight: float32 [4, 1792], replicated, may hold values from -3 to 3
- decay_log: float32 [24], replicated, may hold values from -7 to 0.5
- dt_bias: float32 [24], replicated, may hold values from -4 to -1
- skip_gain: float32 [24], replicated, may hold values from 0.5 to 2
- w_in: bfloat16 [1024, 4120], P('fs'), may hold values from -0.1875 to 0.1875
- w_mout: bfloat16 [1536, 1024], P('fs'), may hold values from -0.15625 to 0.15625
- w_aout: bfloat16 [512, 1024], P('fs'), may hold values from -2 to 2
- w_gu: bfloat16 [1024, 4096], P('fs'), may hold values from -0.1875 to 0.1875
- w_down: bfloat16 [2048, 1024], P('fs'), may hold values from -0.125 to 0.125
- grad_out: bfloat16 [16384, 1024], P(('fs', 'cp', 'ul')), may hold values from -6 to 6
Outputs:
- layer_out: bfloat16 [16384, 1024], P(('fs', 'cp', 'ul'))
- grad_tokens: float32 [16384, 1024], P(('fs', 'cp', 'ul'))
- grad_norm_in: float32 [1024], replicated
- grad_norm_mid: float32 [1024], replicated
- grad_mamba_gain: float32 [1536], replicated
- grad_conv_weight: float32 [4, 1792], replicated
- grad_decay_log: float32 [24], replicated
- grad_dt_bias: float32 [24], replicated
- grad_skip_gain: float32 [24], replicated
- grad_w_in: float32 [1024, 4120], P(('fs', 'cp', 'ul'))
- grad_w_mout: float32 [1536, 1024], P(('fs', 'cp', 'ul'))
- grad_w_aout: float32 [512, 1024], P(('fs', 'cp', 'ul'))
- grad_w_gu: float32 [1024, 4096], P(('fs', 'cp', 'ul'))
- grad_w_down: float32 [2048, 1024], P(('fs', 'cp', 'ul'))
All inputs are finite; a program needn't handle non-finite values.
Results may differ from a plain program's by a relative error of at most 0.019.
Values may be sent and summed in bfloat16 or wider, within the bound.
A program may use at most 256 MiB of HBM per device.

v0:
```python
import jax
import jax.numpy as jnp
import numpy as np
from jax import lax
from jax.sharding import PartitionSpec as P

HM = 24
HP = 64
NS = 128
KW = 4
QUERY_HEAD_TOTAL = 8
KEY_VALUE_HEADS = 2
HEAD_DIMENSION = 64
FF = 2048
SBLK = 256
ABLK = 512
DS = 1536


EPSILON = 1e-05
HIGHEST = lax.Precision.HIGHEST
MASKED = -1e30


def entering_2(shard, axis, join, neutral, backward):
    count = lax.axis_size(axis)
    place = lax.axis_index(axis)
    ahead = count - 1 - place if backward else place
    gathered = jax.tree.map(
        lambda a, kind: lax.all_gather(a.astype(kind), axis),
        shard,
        jax.tree.map(lambda a: jnp.bfloat16 if a.dtype == jnp.float32 else a.dtype, shard),
    )
    state = jax.tree.map(lambda a, e: jnp.zeros_like(a) + jnp.asarray(e, a.dtype), shard, neutral)

    def one(hop, state):
        source = count - 1 - hop if backward else hop
        return join(
            state,
            jax.tree.map(
                lambda a, own: lax.dynamic_index_in_dim(a, source, 0, False).astype(own.dtype),
                gathered,
                shard,
            ),
        )

    return lax.fori_loop(0, ahead, one, state)


def shifted(block, axis, distance):
    devices = range(lax.axis_size(axis))
    route = [(i - distance, i) for i in devices if i - distance in devices]
    return lax.ppermute(block, axis, route)


def rms_norm(values, norm_gain):
    return (
        values * lax.rsqrt(jnp.mean(values * values, axis=-1, keepdims=True) + EPSILON) * norm_gain
    )


def gated_norm(mixed_heads, gate_pre, norm_gain):
    return rms_norm(mixed_heads * jax.nn.silu(gate_pre), norm_gain)


def matmul(left, right):
    return jnp.dot(left, right, preferred_element_type=jnp.float32)


def matmul_tn(left, right):
    return lax.dot_general(
        left, right, (((0,), (0,)), ((), ())), preferred_element_type=jnp.float32
    )


def matmul_nt(left, right):
    return lax.dot_general(
        left, right, (((1,), (1,)), ((), ())), preferred_element_type=jnp.float32
    )


def keep_same(carried_in):
    return carried_in


def causal_conv(extended, weights, length):
    running = extended[0:length] * weights[0]
    for offset in range(1, weights.shape[0]):
        running = running + extended[offset : offset + length] * weights[offset]
    return running


def mixer_prep(extended, conv_local, dt_raw, decay_local, bias_local):
    length, head_count = dt_raw.shape
    x_width = head_count * HP
    convolved = jax.nn.silu(causal_conv(extended, conv_local, length))
    x_heads = convolved[:, :x_width].reshape(length, head_count, HP)
    b_state = convolved[:, x_width : x_width + NS]
    c_state = convolved[:, x_width + NS :]
    step_size = jax.nn.softplus(dt_raw + bias_local)
    log_decay = -jnp.exp(decay_local) * step_size
    return (x_heads, b_state, c_state, step_size, log_decay)


def ssd_run(x_heads, b_state, c_state, step_size, log_decay, skip_local, initial):
    length, head_count = step_size.shape
    blocks = length // SBLK
    lower_mask = jnp.tril(jnp.ones((SBLK, SBLK), dtype=bool))

    def one_block(state_now, pieces):
        x_blk, b_blk, c_blk, step_blk, log_blk = pieces
        cumulative = jnp.cumsum(log_blk, axis=0)
        decay_grid = jnp.exp(
            jnp.where(
                lower_mask[:, :, None], cumulative[:, None, :] - cumulative[None, :, :], MASKED
            )
        )
        inner_prod = jnp.dot(c_blk, b_blk.T, precision=HIGHEST)
        within = jnp.einsum(
            "tsh,shp->thp",
            inner_prod[:, :, None] * decay_grid * step_blk[None, :, :],
            x_blk,
            precision=HIGHEST,
        )
        carried = (
            jnp.einsum("tn,hpn->thp", c_blk, state_now, precision=HIGHEST)
            * jnp.exp(cumulative)[:, :, None]
        )
        tail_weight = jnp.exp(cumulative[-1:] - cumulative) * step_blk
        updated = state_now * jnp.exp(cumulative[-1])[:, None, None] + jnp.einsum(
            "sh,shp,sn->hpn", tail_weight, x_blk, b_blk, precision=HIGHEST
        )
        return (updated, within + carried)

    pieces = (
        x_heads.reshape(blocks, SBLK, head_count, HP),
        b_state.reshape(blocks, SBLK, NS),
        c_state.reshape(blocks, SBLK, NS),
        step_size.reshape(blocks, SBLK, head_count),
        log_decay.reshape(blocks, SBLK, head_count),
    )
    outputs = lax.scan(one_block, initial, pieces)[1]
    return outputs.reshape(length, head_count, HP) + skip_local[None, :, None] * x_heads


def mixer_out(extended, conv_local, dt_raw, decay_local, bias_local, skip_local, initial):
    x_heads, b_state, c_state, step_size, log_decay = mixer_prep(
        extended, conv_local, dt_raw, decay_local, bias_local
    )
    return ssd_run(x_heads, b_state, c_state, step_size, log_decay, skip_local, initial)


def mixer_state(extended, conv_local, dt_raw, decay_local, bias_local):
    x_heads, b_state, c_state, step_size, log_decay = mixer_prep(
        extended, conv_local, dt_raw, decay_local, bias_local
    )
    cumulative = jnp.cumsum(log_decay, axis=0)
    tail_weight = jnp.exp(cumulative[-1:] - cumulative) * step_size
    final_state = jnp.einsum("th,thp,tn->hpn", tail_weight, x_heads, b_state, precision=HIGHEST)
    return (jnp.exp(cumulative[-1]), final_state)


def link_states(earlier, later):
    return (earlier[0] * later[0], later[0][:, None, None] * earlier[1] + later[1])


def chain_states(decays, states, backward):
    identity = (jnp.ones_like(decays), jnp.zeros_like(states))
    return entering_2((decays, states), "cp", link_states, identity, backward)[1]


def shards(
    tokens,
    norm_in,
    norm_mid,
    mamba_gain,
    conv_weight,
    decay_log,
    dt_bias,
    skip_gain,
    w_in,
    w_mout,
    w_aout,
    w_gu,
    w_down,
    grad_out,
):
    single_float = jnp.float32
    bf16 = jnp.bfloat16
    head_grouping = lax.axis_size("ul")
    seq_parts = lax.axis_size("cp")
    group_rank = lax.axis_index("ul")
    part_rank = lax.axis_index("cp")
    token_rows = tokens.shape[0]
    length = head_grouping * token_rows
    seq_len = seq_parts * length
    mamba_local = HM // head_grouping
    query_local = QUERY_HEAD_TOTAL // head_grouping
    sharing_count = QUERY_HEAD_TOTAL // KEY_VALUE_HEADS
    key_value_resident = max(1, query_local // sharing_count)
    per_copy = query_local // key_value_resident
    x_width = mamba_local * HP
    q_width = query_local * HEAD_DIMENSION
    kv_width = key_value_resident * HEAD_DIMENSION
    replicate_heads = np.array(
        [
            rank_id * query_local // sharing_count + slot_id
            for rank_id in range(head_grouping)
            for slot_id in range(key_value_resident)
        ]
    )
    copy_table = (
        (replicate_heads[:, None] == np.arange(KEY_VALUE_HEADS)[None, :])
        .astype(np.float32)
        .reshape(head_grouping, key_value_resident, KEY_VALUE_HEADS)
    )
    full_in, full_mout, full_aout, full_gu, full_down = (
        lax.all_gather(w_in, "fs", axis=0, tiled=True),
        lax.all_gather(w_mout, "fs", axis=0, tiled=True),
        lax.all_gather(w_aout, "fs", axis=0, tiled=True),
        lax.all_gather(w_gu, "fs", axis=0, tiled=True),
        lax.all_gather(w_down, "fs", axis=0, tiled=True),
    )
    resid_in = tokens.astype(single_float)
    normed_f, in_back = jax.vjp(rms_norm, resid_in, norm_in)
    normed_in = normed_f.astype(bf16)
    projected = matmul(normed_in, full_in)
    gate_pre = projected[:, :DS]
    reduced_projection = projected[:, DS:].astype(bf16)
    query_begin = DS + 2 * NS + HM
    x_send = reduced_projection[:, 0:DS].reshape(token_rows, head_grouping, x_width)
    bc_send = jnp.broadcast_to(
        reduced_projection[:, DS : DS + 2 * NS][:, None, :], (token_rows, head_grouping, 2 * NS)
    )
    dt_send = reduced_projection[:, DS + 2 * NS : query_begin].reshape(
        token_rows, head_grouping, mamba_local
    )
    q_send = reduced_projection[
        :, query_begin : query_begin + QUERY_HEAD_TOTAL * HEAD_DIMENSION
    ].reshape(token_rows, head_grouping, q_width)
    key_value_heads = reduced_projection[
        :, query_begin + QUERY_HEAD_TOTAL * HEAD_DIMENSION :
    ].reshape(token_rows, 2, KEY_VALUE_HEADS, HEAD_DIMENSION)[:, :, replicate_heads]
    kv_send = (
        key_value_heads.reshape(token_rows, 2, head_grouping, kv_width)
        .transpose(0, 2, 1, 3)
        .reshape(token_rows, head_grouping, 2 * kv_width)
    )
    slab = jnp.concatenate([x_send, bc_send, q_send, kv_send], axis=2)
    slab_in, dt_in = (
        lax.all_to_all(slab, "ul", split_axis=1, concat_axis=0, tiled=True),
        lax.all_to_all(dt_send, "ul", split_axis=1, concat_axis=0, tiled=True),
    )
    slab_in = slab_in.reshape(length, slab.shape[2])
    dt_raw = dt_in.reshape(length, mamba_local).astype(single_float)
    conv_width = x_width + 2 * NS
    conv_in = slab_in[:, :conv_width]
    query_head_rows = slab_in[:, conv_width : conv_width + q_width].reshape(
        length, key_value_resident, per_copy, HEAD_DIMENSION
    )
    k_local = slab_in[:, conv_width + q_width : conv_width + q_width + kv_width]
    v_local = slab_in[:, conv_width + q_width + kv_width :]
    rim_prev = shifted(conv_in[length - (KW - 1) :], "cp", 1)
    extended = jnp.concatenate([rim_prev, conv_in], axis=0).astype(single_float)
    conv_local = jnp.concatenate(
        [
            lax.dynamic_slice_in_dim(conv_weight[:, :DS], group_rank * x_width, x_width, 1),
            conv_weight[:, DS:],
        ],
        axis=1,
    )
    decay_local = lax.dynamic_slice_in_dim(decay_log, group_rank * mamba_local, mamba_local)
    bias_local = lax.dynamic_slice_in_dim(dt_bias, group_rank * mamba_local, mamba_local)
    skip_local = lax.dynamic_slice_in_dim(skip_gain, group_rank * mamba_local, mamba_local)
    (decays, final_state), state_back = jax.vjp(
        mixer_state, extended, conv_local, dt_raw, decay_local, bias_local
    )
    entering = chain_states(decays, final_state, False)
    mixed_heads, out_back = jax.vjp(
        mixer_out, extended, conv_local, dt_raw, decay_local, bias_local, skip_local, entering
    )
    mixed_low = mixed_heads.reshape(length, x_width).astype(bf16)
    k_whole, v_whole = (
        lax.all_gather(k_local, "cp", axis=0, tiled=True),
        lax.all_gather(v_local, "cp", axis=0, tiled=True),
    )
    key_blocks = seq_len // ABLK
    k_blocks = k_whole.reshape(key_blocks, ABLK, key_value_resident, HEAD_DIMENSION)
    v_blocks = v_whole.reshape(key_blocks, ABLK, key_value_resident, HEAD_DIMENSION)
    starts = jnp.arange(key_blocks, dtype=jnp.int32) * ABLK
    query_pos = part_rank * length + jnp.arange(length, dtype=jnp.int32)
    last_query = part_rank * length + length - 1
    logit_scale = HEAD_DIMENSION ** (-0.5)
    stat_shape = (length, key_value_resident, per_copy)

    def block_scores(key_block_slice, key_start):
        raw_scores = (
            jnp.einsum(
                "jnue,xne->jnux",
                query_head_rows,
                key_block_slice,
                preferred_element_type=single_float,
            )
            * logit_scale
        )
        visible = query_pos[:, None] >= (key_start + jnp.arange(ABLK, dtype=jnp.int32))[None, :]
        return jnp.where(visible[:, None, None, :], raw_scores, MASKED)

    def max_step(carry_pair, pieces):
        key_block_slice, key_start = pieces

        def max_live(state_pair):
            scored = block_scores(key_block_slice, key_start)
            top_new = jnp.maximum(state_pair[0], jnp.max(scored, axis=-1))
            exp_sum = state_pair[1] * jnp.exp(state_pair[0] - top_new) + jnp.sum(
                jnp.exp(scored - top_new[..., None]), axis=-1
            )
            return (top_new, exp_sum)

        return (lax.cond(key_start <= last_query, max_live, keep_same, carry_pair), None)

    top_score, exp_total = lax.scan(
        max_step,
        (jnp.full(stat_shape, MASKED, single_float), jnp.zeros(stat_shape, single_float)),
        (k_blocks, starts),
    )[0]
    log_total = top_score + jnp.log(exp_total)

    def out_step(running_out, pieces):
        key_block_slice, value_block_slice, key_start = pieces

        def out_live(out_in):
            probability_block = jnp.exp(
                block_scores(key_block_slice, key_start) - log_total[..., None]
            ).astype(bf16)
            return out_in + jnp.einsum(
                "lmsn,nmp->lmsp",
                probability_block,
                value_block_slice,
                preferred_element_type=single_float,
            )

        return (lax.cond(key_start <= last_query, out_live, keep_same, running_out), None)

    attended = lax.scan(
        out_step,
        jnp.zeros((length, key_value_resident, per_copy, HEAD_DIMENSION), single_float),
        (k_blocks, v_blocks, starts),
    )[0]
    attended_low = attended.reshape(length, q_width).astype(bf16)
    mixed_tok, attended_tok = (
        lax.all_to_all(
            mixed_low.reshape(head_grouping, token_rows, 1, x_width),
            "ul",
            split_axis=0,
            concat_axis=2,
            tiled=True,
        ),
        lax.all_to_all(
            attended_low.reshape(head_grouping, token_rows, 1, q_width),
            "ul",
            split_axis=0,
            concat_axis=2,
            tiled=True,
        ),
    )
    mixed_tok = mixed_tok.reshape(token_rows, DS)
    attended_tok = attended_tok.reshape(token_rows, QUERY_HEAD_TOTAL * HEAD_DIMENSION)
    branch_f, gate_back = jax.vjp(gated_norm, mixed_tok.astype(single_float), gate_pre, mamba_gain)
    branch_low = branch_f.astype(bf16)
    resid_mid = resid_in + matmul(branch_low, full_mout) + matmul(attended_tok, full_aout)
    normed_mid_f, mid_back = jax.vjp(rms_norm, resid_mid, norm_mid)
    normed_mid = normed_mid_f.astype(bf16)
    gate_up = matmul(normed_mid, full_gu)
    gate_half = gate_up[:, :FF]
    up_half = gate_up[:, FF:]
    sigmoid_gate = jax.nn.sigmoid(gate_half)
    hidden = (gate_half * sigmoid_gate * up_half).astype(bf16)
    layer_out = (resid_mid + matmul(hidden, full_down)).astype(bf16)
    cotangent = grad_out.astype(single_float)
    grad_down = matmul_tn(hidden, grad_out)
    grad_hidden = matmul_nt(grad_out, full_down)
    grad_gate = grad_hidden * up_half * sigmoid_gate * (1.0 + gate_half * (1.0 - sigmoid_gate))
    grad_up = grad_hidden * gate_half * sigmoid_gate
    grad_gate_up = jnp.concatenate([grad_gate, grad_up], axis=1).astype(bf16)
    grad_gu = matmul_tn(normed_mid, grad_gate_up)
    resid_back, grad_norm_mid = mid_back(matmul_nt(grad_gate_up, full_gu))
    grad_resid = cotangent + resid_back
    resid_low = grad_resid.astype(bf16)
    grad_mout = matmul_tn(branch_low, resid_low)
    grad_aout = matmul_tn(attended_tok, resid_low)
    grad_mixed, grad_gate_pre, grad_mamba_gain = gate_back(matmul_nt(resid_low, full_mout))
    grad_attended = matmul_nt(resid_low, full_aout)
    mixed_grad_in, attended_grad_in = (
        lax.all_to_all(
            grad_mixed.astype(bf16).reshape(token_rows, head_grouping, x_width),
            "ul",
            split_axis=1,
            concat_axis=0,
            tiled=True,
        ),
        lax.all_to_all(
            grad_attended.astype(bf16).reshape(token_rows, head_grouping, q_width),
            "ul",
            split_axis=1,
            concat_axis=0,
            tiled=True,
        ),
    )
    grad_heads = mixed_grad_in.reshape(length, mamba_local, HP).astype(single_float)
    attention_gradient = attended_grad_in.reshape(
        length, key_value_resident, per_copy, HEAD_DIMENSION
    )
    row_delta = jnp.sum(attention_gradient.astype(single_float) * attended, axis=-1)

    def back_step(grad_query, pieces):
        key_block_slice, value_block_slice, key_start = pieces

        def back_live(query_in):
            probability_block = jnp.exp(
                block_scores(key_block_slice, key_start) - log_total[..., None]
            )
            probability_reduced = probability_block.astype(bf16)
            grad_value = jnp.einsum(
                "caoe,caoj->eaj",
                probability_reduced,
                attention_gradient,
                preferred_element_type=single_float,
            )
            probability_gradient = jnp.einsum(
                "jnue,xne->jnux",
                attention_gradient,
                value_block_slice,
                preferred_element_type=single_float,
            )
            score_gradient = (
                probability_block * (probability_gradient - row_delta[..., None])
            ).astype(bf16)
            query_out = (
                query_in
                + jnp.einsum(
                    "lmsn,nmp->lmsp",
                    score_gradient,
                    key_block_slice,
                    preferred_element_type=single_float,
                )
                * logit_scale
            )
            grad_key = (
                jnp.einsum(
                    "caoe,caoj->eaj",
                    score_gradient,
                    query_head_rows,
                    preferred_element_type=single_float,
                )
                * logit_scale
            )
            return (
                query_out,
                jnp.concatenate(
                    [grad_key.reshape(ABLK, kv_width), grad_value.reshape(ABLK, kv_width)], axis=1
                ),
            )

        def skipped(query_in):
            return (query_in, jnp.zeros((ABLK, 2 * kv_width), single_float))

        return lax.cond(key_start <= last_query, back_live, skipped, grad_query)

    grad_query, key_terms = lax.scan(
        back_step,
        jnp.zeros((length, key_value_resident, per_copy, HEAD_DIMENSION), single_float),
        (k_blocks, v_blocks, starts),
    )
    key_grads = lax.psum_scatter(
        key_terms.reshape(seq_len, 2 * kv_width).astype(jnp.bfloat16),
        "cp",
        scatter_dimension=0,
        tiled=True,
    ).astype(jnp.float32)
    (
        grad_ext_a,
        grad_conv_a,
        grad_dt_a,
        grad_decay_a,
        grad_bias_a,
        grad_skip_local,
        grad_entering,
    ) = out_back(grad_heads)
    passed_back = chain_states(decays, grad_entering, True)
    grad_decays = jnp.sum(passed_back * entering, axis=(1, 2))
    grad_ext_b, grad_conv_b, grad_dt_b, grad_decay_b, grad_bias_b = state_back(
        (grad_decays, passed_back)
    )
    grad_ext = grad_ext_a + grad_ext_b
    rim_next = shifted(grad_ext[: KW - 1], "cp", -1)
    grad_conv_in = grad_ext[KW - 1 :] + jnp.concatenate(
        [jnp.zeros((length - (KW - 1), conv_width), single_float), rim_next], axis=0
    )
    grad_dt = grad_dt_a + grad_dt_b
    back_slab = jnp.concatenate(
        [grad_conv_in, grad_query.reshape(length, q_width), key_grads], axis=1
    ).astype(bf16)
    slab_back, dt_back = (
        lax.all_to_all(
            back_slab.reshape(length, 1, back_slab.shape[1]),
            "ul",
            split_axis=0,
            concat_axis=1,
            tiled=True,
        ),
        lax.all_to_all(
            grad_dt.astype(bf16).reshape(length, 1, mamba_local),
            "ul",
            split_axis=0,
            concat_axis=1,
            tiled=True,
        ),
    )
    grad_x = slab_back[:, :, :x_width].reshape(token_rows, DS)
    grad_bc = jnp.sum(slab_back[:, :, x_width:conv_width].astype(single_float), axis=1).astype(bf16)
    grad_q = slab_back[:, :, conv_width : conv_width + q_width].reshape(
        token_rows, QUERY_HEAD_TOTAL * HEAD_DIMENSION
    )
    grad_copies = (
        slab_back[:, :, conv_width + q_width :]
        .reshape(token_rows, head_grouping, 2, key_value_resident, HEAD_DIMENSION)
        .astype(single_float)
    )
    grad_kv = (
        jnp.einsum("trcsd,rsh->tchd", grad_copies, jnp.asarray(copy_table), precision=HIGHEST)
        .astype(bf16)
        .reshape(token_rows, 2 * KEY_VALUE_HEADS * HEAD_DIMENSION)
    )
    grad_dt_tok = dt_back.reshape(token_rows, HM)
    grad_proj = jnp.concatenate(
        [grad_gate_pre.astype(bf16), grad_x, grad_bc, grad_dt_tok, grad_q, grad_kv], axis=1
    )
    grad_in = matmul_tn(normed_in, grad_proj)
    tokens_back, grad_norm_in = in_back(matmul_nt(grad_proj, full_in))
    grad_tokens = grad_resid + tokens_back
    grad_conv_local = grad_conv_a + grad_conv_b
    conv_full = jnp.concatenate(
        [
            lax.dynamic_update_slice_in_dim(
                jnp.zeros((KW, DS), single_float),
                grad_conv_local[:, :x_width],
                group_rank * x_width,
                1,
            ),
            grad_conv_local[:, x_width:],
        ],
        axis=1,
    )
    decay_full = lax.dynamic_update_slice_in_dim(
        jnp.zeros((HM,), single_float), grad_decay_a + grad_decay_b, group_rank * mamba_local, 0
    )
    bias_full = lax.dynamic_update_slice_in_dim(
        jnp.zeros((HM,), single_float), grad_bias_a + grad_bias_b, group_rank * mamba_local, 0
    )
    skip_full = lax.dynamic_update_slice_in_dim(
        jnp.zeros((HM,), single_float), grad_skip_local, group_rank * mamba_local, 0
    )
    summed_small = lax.psum(
        (grad_norm_in, grad_norm_mid, grad_mamba_gain, conv_full, decay_full, bias_full, skip_full),
        ("fs", "cp", "ul"),
    )
    reduced = (
        lax.psum_scatter(grad_in, ("fs", "cp", "ul"), scatter_dimension=0, tiled=True),
        lax.psum_scatter(grad_mout, ("fs", "cp", "ul"), scatter_dimension=0, tiled=True),
        lax.psum_scatter(grad_aout, ("fs", "cp", "ul"), scatter_dimension=0, tiled=True),
        lax.psum_scatter(grad_gu, ("fs", "cp", "ul"), scatter_dimension=0, tiled=True),
        lax.psum_scatter(grad_down, ("fs", "cp", "ul"), scatter_dimension=0, tiled=True),
    )
    return (
        layer_out,
        grad_tokens,
        summed_small[0],
        summed_small[1],
        summed_small[2],
        summed_small[3],
        summed_small[4],
        summed_small[5],
        summed_small[6],
        reduced[0],
        reduced[1],
        reduced[2],
        reduced[3],
        reduced[4],
    )


def solution(mesh):
    in_specs = (
        P(("fs", "cp", "ul"), None),
        P(),
        P(),
        P(),
        P(),
        P(),
        P(),
        P(),
        P("fs", None),
        P("fs", None),
        P("fs", None),
        P("fs", None),
        P("fs", None),
        P(("fs", "cp", "ul"), None),
    )
    out_specs = (
        P(("fs", "cp", "ul"), None),
        P(("fs", "cp", "ul"), None),
        P(),
        P(),
        P(),
        P(),
        P(),
        P(),
        P(),
        P(("fs", "cp", "ul"), None),
        P(("fs", "cp", "ul"), None),
        P(("fs", "cp", "ul"), None),
        P(("fs", "cp", "ul"), None),
        P(("fs", "cp", "ul"), None),
    )
    return jax.shard_map(shards, mesh=mesh, in_specs=in_specs, out_specs=out_specs, check_vma=False)
```

profile of v0, /device:TPU:1, one launch (start us, length us, event | category | flops | bytes accessed | tf_op | source)
XLA Modules:
  0.0 2298.2 jit_solution(15857026506690501211)
XLA Ops:
  11.1 88.8 %all-gather.9.cloned.1.call-done = bf16[1024,4120]{0,1:T(8,128)(2,1)} async-done(((bf16[256,4120]{0,1:T(8,128)(2,1)}), bf16[1024,4120]{0,1:T(8,128)(2,1)}) %all-gather.9.cloned.1.call-update) | async-done | bytes 8437776 | tf_op jit(solution)/shard_map/all_gather | solution.py:218
  99.9 6.3 fusion.245
  106.8 5.8 all-to-all-start
  126.1 8.6 all-gather.2
  143.5 12.2 all_gather.45
  156.2 13.8 while.141
  182.0 19.8 all-gather
  205.4 104.8 %while.144 = (s32[]{:T(128)}, f32[3,64,128]{2,1,0:T(8,128)S(1)}, f32[4,256,3,64]{1,0,3,2:T(4,128)}, f32[4,256,256,3]{2,1,3,0:T(8,128)}, f32[4,128,256]{1,2,0:T(8...) while((s32[]{:T(128)}, f32[3,64,128]{2,1,0:T(8,128)S(1)}, ...), condition=%wide.region_8.10_spmd.clone.clone, body=%wide.region_5.9_spmd.clone.clone.sunk | while | flops 404571648 | bytes 7627489 | solution.py:142
  316.1 8.5 all-to-all-start.2
  324.6 14.7 all_gather.44
  341.7 15.1 while.142
  357.6 6.4 all-to-all-start.3
  372.8 6.0 fusion.235
  409.8 31.3 %while.143 = (s32[]{:T(128)}, f32[1024,1,1,64]{0,3,2,1:T(8,128)S(1)}, bf16[8,512,128]{1,2,0:T(8,128)(2,1)}, s32[8]{0:T(128)}, s32[]{:T(128)}, /*index=5*/bf16[8,...) while((s32[]{:T(128)}, ...), condition=%wide.region_40.42_spmd.clone, body=%wide.region_37.41_spmd.clone.sunk | while | flops 340198912 | bytes 11368719 | solution.py:470
  419.6 5.5 conditional.11
  454.2 133.0 %while.145 = (s32[]{:T(128)}, f32[3,64,128]{2,1,0:T(8,128)S(1)}, f32[4,256,3,64]{1,0,3,2:T(4,128)}, f32[4,256,128]{2,1,0:T(8,128)}, f32[4,256,128]{2,1,0:T(8,128...) while((s32[]{:T(128)}, f32[3,64,128]{2,1,0:T(8,128)S(1)}, ...), condition=%wide.region_33.35_spmd.clone, body=%wide.region_23.34_spmd.clone.sunk | while | flops 807968256 | bytes 9659709 | solution.py:142
  587.2 58.4 %all-gather.1 = bf16[12,64,128]{2,1,0:T(8,128)(2,1)} all-gather(bf16[3,64,128]{2,1,0:T(8,128)(2,1)S(1)} %convert_element_type.245), channel_id=3, replica_groups=mesh['fs'=4,'cp'=4,'ul'=8] {'cp'}, dimensions={0}, use_global_device_ids=true | all-gather | bytes 245760 | tf_op jit(solution)/shard_map/all_gather | solution.py:30
  664.8 6.2 multiply_reduce_fusion.7
  671.0 6.8 broadcast_multiply_fusion
  690.1 8.7 add_add_fusion
  701.2 7.3 all-to-all-start.7
  725.7 11.6 all-to-all-done.6
  746.3 8.4 fusion.204
  761.1 9.7 fusion.189
  775.4 382.4 %fusion.10 = f32[16,1024]{1,0:T(8,128)S(1)} fusion(f32[1536,1024]{1,0:T(8,128)} %fusion.246), kind=kCustom, calls=%all-reduce-scatter | all-reduce-scatter fusion | flops 2097153 | bytes 6356992
  1169.5 13.7 collective-permute-start.24
  1183.2 6.1 collective-permute-start.23
  1197.9 5.8 collective-permute-start.19
  1256.4 49.0 %concatenate.55 = f32[524,1024]{1,0:T(8,128)} concatenate(f32[12,1024]{1,0:T(8,128)S(1)} %collective-permute-done.33, f32[16,1024]{1,0:T(8,128)S(1)} %collective-permute-done.32, f32[16,1024]{1,0:T(8,128)S(1)} %collective-permute-done.31, f32[16,1024]{1,0:T(8,128)S(1)} %collective-permute-done.30, f32[16,1024]{1,0:T(8,128)S(1)} %collective-permute-done.29, ...), dimensions={0} | concatenate | bytes 4292608
  1313.3 68.3 %all-reduce.30 = (f32[1024]{0:T(1024)}, f32[1024]{0:T(1024)}, f32[1536]{0:T(1024)}, f32[4,1792]{1,0:T(4,128)}, f32[24]{0:T(128)}, /*index=5*/f32[24]{0:T(128)}, f32[24]{0:T(128)}) all-reduce(f32[1024]{0:T(1024)S(1)} %get-tuple-element.2231, f32[1024]{0:T(1024)S(1)} %copy-done.81, ...), channel_id=1, replica_groups=mesh['fs'=4,'cp'=4,'ul'=8] {'fs','cp','ul'}, use_global_device_ids=true, to_apply=%region_49.51 | all-reduce | flops 10824 | bytes 86592 | tf_op jit(solution)/shard_map/psum | solution.py:564
  1385.6 243.9 %reduce-scatter.10.cloned.1.call-done = f32[16,1024]{1,0:T(8,128)} async-done(((f32[2048,1024]{1,0:T(8,128)}), f32[16,1024]{1,0:T(8,128)}) %reduce-scatter.10.cloned.1.call-update) | async-done | bytes 65552 | tf_op jit(solution)/shard_map/reduce_scatter | solution.py:573
  1629.5 661.7 %reduce-scatter.8.cloned.1.call-done = f32[8,4096]{1,0:T(8,128)} async-done(((f32[1024,4096]{1,0:T(8,128)}), f32[8,4096]{1,0:T(8,128)}) %reduce-scatter.8.cloned.1.call-update) | async-done | bytes 131088 | tf_op jit(solution)/shard_map/reduce_scatter | solution.py:572
  (957 shorter events, 558.0 us)
Async XLA Ops:
  7.2 92.7 %all-gather.9.cloned.1.call-start = ((), (), s32[]{:S(2)}) async-start(), calls=%async_computation.11 | async-start | bytes 10547200 | tf_op jit(solution)/shard_map/all_gather | solution.py:218
  8.0 359.4 %all-gather.11.cloned.1.call-start = ((), (), s32[]{:S(2)}) async-start(), calls=%async_computation.12 | async-start | bytes 3932160 | tf_op jit(solution)/shard_map/all_gather | solution.py:219
  8.7 362.2 %all-gather.13.cloned.1.call-start = ((), (), s32[]{:S(2)}) async-start(), calls=%async_computation.13 | async-start | bytes 1310720 | tf_op jit(solution)/shard_map/all_gather | solution.py:220
  9.5 363.3 %all-gather.15.cloned.1.call-start = ((), (), s32[]{:S(2)}) async-start(), calls=%async_computation.14 | async-start | bytes 10485760 | tf_op jit(solution)/shard_map/all_gather | solution.py:221
  10.0 368.8 %all-gather.17.cloned.1.call-start = ((), (), s32[]{:S(2)}) async-start(), calls=%async_computation.15 | async-start | bytes 5242880 | tf_op jit(solution)/shard_map/all_gather | solution.py:222
  117.3 22.1 all-to-all-start.1
  140.3 30.6 %collective-permute-start = (bf16[3,448]{1,0:T(4,128)(2,1)S(1)}, bf16[3,448]{1,0:T(4,128)(2,1)S(1)}, u32[]{:S(2)}, u32[]{:S(2)}) collective-permute-start(bf16[3,448]{1,0:T(4,128)(2,1)S(1)} %slice.229), channel_id=1, source_target_pairs={{0,8},{8,16},{16,24},{1,9},{9,17},{17,25},{2,10},{10,18},{18,26},{... | collective-permute-start | bytes 8072 | tf_op jit(solution)/shard_map/ppermute | solution.py:53
  316.1 41.5 %all-to-all-start.2 = ((bf16[8,128,1,192]{1,3,2,0:T(8,128)(2,1)}), bf16[8,128,1,192]{1,3,2,0:T(8,128)(2,1)S(1)}, u32[]{:S(2)}, u32[]{:S(2)}) async-start(bf16[8,128,1,192]{1,3,2,0:T(8,128)(2,1)} %copy.516), calls=%async_computation.2 | async-start | bytes 786432 | tf_op jit(solution)/shard_map/all_to_all | solution.py:352
  403.3 40.9 %all-to-all-start.4 = ((bf16[128,8,192]{0,2,1:T(8,128)(2,1)}), bf16[128,8,192]{0,2,1:T(8,128)(2,1)}, u32[]{:S(2)}, u32[]{:S(2)}) async-start(bf16[128,8,192]{0,2,1:T(8,128)(2,1)} %bitcast.862), calls=%async_computation.4 | async-start | bytes 786432 | tf_op jit(solution)/shard_map/all_to_all | solution.py:395
  408.1 302.2 %reduce-scatter.6.cloned.1.call-start = ((), (), s32[]{:S(2)}) async-start(), calls=%async_computation.16 | async-start | bytes 1310720 | tf_op jit(solution)/shard_map/reduce_scatter | solution.py:475
  681.8 26.7 %collective-permute-start.1 = (f32[3,448]{1,0:T(4,128)S(1)}, f32[3,448]{1,0:T(4,128)S(1)}, u32[]{:S(2)}, u32[]{:S(2)}) collective-permute-start(f32[3,448]{1,0:T(4,128)S(1)} %add_add_fusion.4), channel_id=1, source_target_pairs={{8,0},{16,8},{24,16},{9,1},{17,9},{25,17},{10,2},{18,10},{26,18},{... | collective-permute-start | bytes 16136 | tf_op jit(solution)/shard_map/ppermute | solution.py:53
  714.5 22.8 all-to-all-start.6
  719.4 663.3 %all-reduce.34.cloned.1.call-start = ((), (), s32[]{:S(2)}) async-start(), calls=%async_computation.19 | async-start | bytes 38797312
  754.8 874.8 %reduce-scatter.10.cloned.1.call-start = ((), (), s32[]{:S(2)}) async-start(), calls=%async_computation.18 | async-start | bytes 8454144 | tf_op jit(solution)/shard_map/reduce_scatter | solution.py:573
  760.4 1530.8 %reduce-scatter.8.cloned.1.call-start = ((), (), s32[]{:S(2)}) async-start(), calls=%async_computation.17 | async-start | bytes 16908288 | tf_op jit(solution)/shard_map/reduce_scatter | solution.py:572
  1164.3 18.9 collective-permute-start.28
  1165.6 23.8 %collective-permute-start.27 = (f32[16,1024]{1,0:T(8,128)S(1)}, f32[16,1024]{1,0:T(8,128)S(1)}, u32[]{:S(2)}, u32[]{:S(2)}) collective-permute-start(f32[16,1024]{1,0:T(8,128)S(1)} %fusion.10), channel_id=1, source_target_pairs={{0,26},{1,27},{2,28},{3,29},{4,30},{5,31},{6,32},{7,33},{8,34},{9,... | collective-permute-start | bytes 196616
  1166.9 25.3 %collective-permute-start.26 = (f32[16,1024]{1,0:T(8,128)S(1)}, f32[16,1024]{1,0:T(8,128)S(1)}, u32[]{:S(2)}, u32[]{:S(2)}) collective-permute-start(f32[16,1024]{1,0:T(8,128)S(1)} %fusion.10), channel_id=1, source_target_pairs={{0,25},{1,26},{2,27},{3,28},{4,29},{5,30},{6,31},{7,32},{8,33},{9,... | collective-permute-start | bytes 196616
  1168.2 26.2 %collective-permute-start.25 = (f32[16,1024]{1,0:T(8,128)S(1)}, f32[16,1024]{1,0:T(8,128)S(1)}, u32[]{:S(2)}, u32[]{:S(2)}) collective-permute-start(f32[16,1024]{1,0:T(8,128)S(1)} %fusion.10), channel_id=1, source_target_pairs={{0,24},{1,25},{2,26},{3,27},{4,28},{5,29},{6,30},{7,31},{8,32},{9,... | collective-permute-start | bytes 196616
  1169.5 28.4 %collective-permute-start.24 = (f32[16,1024]{1,0:T(8,128)S(1)}, f32[16,1024]{1,0:T(8,128)S(1)}, u32[]{:S(2)}, u32[]{:S(2)}) collective-permute-start(f32[16,1024]{1,0:T(8,128)S(1)} %fusion.10), channel_id=1, source_target_pairs={{0,23},{1,24},{2,25},{3,26},{4,27},{5,28},{6,29},{7,30},{8,31},{9,... | collective-permute-start | bytes 196616
  1183.2 20.5 collective-permute-start.23
  1189.4 15.6 collective-permute-start.22
  1206.4 15.4 collective-permute-start.16
  1207.7 16.0 collective-permute-start.15
  1212.0 15.5 collective-permute-start.14
  1214.6 14.8 collective-permute-start.13
  1223.7 14.2 collective-permute-start.10
  1229.4 15.4 collective-permute-start.8
  1231.6 15.4 collective-permute-start.7
  1235.4 19.8 collective-permute-start.6
  1237.9 17.2 collective-permute-start.5
  1240.7 14.4 collective-permute-start.4
  (144 other events, 2816.1 us)
Sparse Core Ops, SparseCore 0:
  9.7 90.1 all-gather.8
  101.5 40.7 all-gather.10
  144.0 23.2 all-gather.12
  168.8 84.3 all-gather.14
  254.7 49.2 all-gather.16
  443.5 70.3 reduce-scatter.5
  754.9 226.2 all-reduce.33
  984.2 645.2 reduce-scatter.9
  1632.5 658.7 reduce-scatter.7
where the time goes:
time: 2320 us; the launch traced here: 2300 us
  waiting for transfers between devices  1020 us (44%)
  blocking collectives  564 us (24%)
  local copies, waits for them, and re-layouts  243 us (10%)
  matrix products  178 us (8%)
  starting transfers between devices  145 us (6%)
  other arithmetic  118 us (5%)
    reduce_scatter x1, waiting for transfers between devices, shards(): lax.psum_scatter(grad_gu, ('fs', 'cp', 'ul'), scatter_dimension=0, tiled=...  662 us
    unnamed x1, blocking collectives  382 us
    reduce_scatter x1, waiting for transfers between devices, shards(): lax.psum_scatter(grad_down, ('fs', 'cp', 'ul'), scatter_dimension=0, tile...  244 us
    unnamed x33, starting transfers between devices  93 us
    all_gather x1, waiting for transfers between devices, shards(): lax.all_gather(w_in, 'fs', axis=0, tiled=True)  88.8 us
    all_gather x3, blocking collectives, entering_2(): lax.all_gather(a.astype(kind), axis)  86.9 us
    unnamed x268, local copies, waits for them, and re-layouts  82.6 us
    psum x1, blocking collectives, shards(): lax.psum((grad_norm_in, grad_norm_mid, grad_mamba_gain, conv_full, decay_...  68.3 us
  transfers between devices with their start and end apart: 51, of which 7 were waited for; matrix products, arithmetic and copies ran while one was open for 38% of the time, Pallas kernels for 0%

commit v1 on v0

v1 whole, which is shorter than its diff:
```python
import functools
import jax
import jax.numpy as jnp
from jax import lax
from jax.experimental import pallas as pl
from jax.experimental.pallas import tpu as pltpu
from jax.sharding import Mesh
from jax.sharding import PartitionSpec as P

HP = 64
NS = 128
KW = 4
SBLK = 256
MASKED = -1e30
HIGHEST = lax.Precision.HIGHEST
F32 = jnp.float32
BF16 = jnp.bfloat16
VMEM_LIMIT = 56 * 1024 * 1024
XW = 192
CW = 448
HALO = 16
DT_AT = 640
Q_AT = 448
KV_AT = 512


def nn(a, b, precision=None):
    return lax.dot_general(
        a, b, (((1,), (0,)), ((), ())), precision=precision, preferred_element_type=F32
    )


def nt(a, b):
    return lax.dot_general(a, b, (((1,), (1,)), ((), ())), preferred_element_type=F32)


def tn(a, b):
    return lax.dot_general(a, b, (((0,), (0,)), ((), ())), preferred_element_type=F32)


def iota(shape, dim):
    return lax.broadcasted_iota(jnp.int32, shape, dim)


def spread(per_head, rows):
    return jnp.concatenate(
        [jnp.broadcast_to(per_head[:, h : h + 1], (rows, HP)) for h in range(XW // HP)], axis=1
    )


def head_sum_matrix():
    return (iota((XW, 128), 0) // HP == iota((XW, 128), 1)).astype(F32)


def conv_pre(ext, weights, base, lanes=slice(None)):
    pre = ext[pl.ds(base + HALO - 3, SBLK), :] * weights[0:1, :]
    for k in range(1, KW):
        pre = pre + ext[pl.ds(base + HALO - 3 + k, SBLK), :] * weights[k : k + 1, :]
    return pre


def step_and_log(slab, par_ref, base):
    raw = slab[pl.ds(base, SBLK), DT_AT:].astype(F32) + par_ref[1:2, :]
    step = jnp.maximum(raw, 0.0) + jnp.log1p(jnp.exp(-jnp.abs(raw)))
    return raw, step, -jnp.exp(par_ref[0:1, :]) * step


def ssd_forward(slab, halo, taps, par, y_out, state_out, c_out, cum_out, entry_out, ext):
    length = slab.shape[0]
    ext[pl.ds(0, HALO), :] = halo[...].astype(F32)
    ext[pl.ds(HALO, length), :] = slab[:, :CW].astype(F32)
    weights = taps[...]
    lower = iota((SBLK, SBLK), 0) >= iota((SBLK, SBLK), 1)
    tri = lower.astype(F32)
    state_out[...] = jnp.zeros_like(state_out)
    before = jnp.zeros((1, 128), F32)
    for k in range(length // SBLK):
        base = k * SBLK
        pre = conv_pre(ext, weights, base)
        conv = pre * jax.nn.sigmoid(pre)
        b_low = conv[:, :NS].astype(BF16)
        c_low = conv[:, NS : 2 * NS].astype(BF16)
        x = conv[:, 2 * NS :]
        raw, step, log = step_and_log(slab, par, base)
        cum = nn(tri, log, HIGHEST)
        cum_t = cum.T
        u = x * spread(step, SBLK)
        u_low = u.astype(BF16)
        inner = nt(c_low, b_low)
        state = state_out[pl.ds(0, XW), :]
        entry_out[k] = state
        parts = []
        for h in range(XW // HP):
            decay = jnp.exp(
                jnp.where(lower, cum[:, h : h + 1] - cum_t[h : h + 1, :], MASKED)
            )
            parts.append(nn((inner * decay).astype(BF16), u_low[:, h * HP : (h + 1) * HP]))
        carried = nt(c_low, state.astype(BF16)) * spread(jnp.exp(cum), SBLK)
        y_out[pl.ds(base, SBLK), :] = (
            jnp.concatenate(parts, axis=1) + carried + spread(par[2:3, :], 1) * x
        )
        last = cum[SBLK - 1 : SBLK, :]
        tail = (u * spread(jnp.exp(last - cum), SBLK)).astype(BF16)
        shrink = jnp.concatenate(
            [
                jnp.broadcast_to(jnp.exp(last[:, h : h + 1]), (HP, NS))
                for h in range(XW // HP)
            ],
            axis=0,
        )
        state_out[pl.ds(0, XW), :] = state * shrink + tn(tail, b_low)
        c_out[pl.ds(base, SBLK), :] = c_low
        cum_out[pl.ds(base, SBLK), :] = cum + before
        before = before + last
    state_out[pl.ds(XW, 8), :] = jnp.broadcast_to(before, (8, 128))


def ssd_forward_call(slab, halo, taps, par):
    length = slab.shape[0]
    return pl.pallas_call(
        ssd_forward,
        out_shape=(
            jax.ShapeDtypeStruct((length, XW), F32),
            jax.ShapeDtypeStruct((XW + 8, NS), F32),
            jax.ShapeDtypeStruct((length, NS), BF16),
            jax.ShapeDtypeStruct((length, 128), F32),
            jax.ShapeDtypeStruct((length // SBLK, XW, NS), F32),
        ),
        scratch_shapes=[pltpu.VMEM((length + HALO, CW), F32)],
        compiler_params=pltpu.CompilerParams(vmem_limit_bytes=VMEM_LIMIT),
        cost_estimate=pl.CostEstimate(
            flops=8_000_000_000, bytes_accessed=8_000_000, transcendentals=1_000_000
        ),
        name="ssd_forward",
    )(slab, halo, taps, par)


def shrink_rows(log_row):
    return jnp.concatenate(
        [jnp.broadcast_to(jnp.exp(log_row[:, h : h + 1]), (HP, NS)) for h in range(XW // HP)],
        axis=0,
    )


def ssd_join(y, c, cum, near, mid, far, attended, out, entering):
    state = near[pl.ds(0, XW), :] + shrink_rows(near[XW : XW + 1, :]) * (
        mid[pl.ds(0, XW), :] + shrink_rows(mid[XW : XW + 1, :]) * far[pl.ds(0, XW), :]
    )
    entering[...] = state
    state_low = state.astype(BF16)
    rows = y.shape[0]
    for base in range(0, rows, SBLK):
        at = pl.ds(base, SBLK)
        mixed = y[at, :] + nt(c[at, :], state_low) * spread(jnp.exp(cum[at, :]), SBLK)
        out[at, :] = jnp.concatenate([mixed, attended[at, :]], axis=1).astype(BF16)


def ssd_join_call(y, c, cum, near, mid, far, attended):
    return pl.pallas_call(
        ssd_join,
        out_shape=(
            jax.ShapeDtypeStruct((y.shape[0], XW + HP), BF16),
            jax.ShapeDtypeStruct((XW, NS), F32),
        ),
        compiler_params=pltpu.CompilerParams(vmem_limit_bytes=VMEM_LIMIT),
        name="ssd_join",
    )(y, c, cum, near, mid, far, attended)


def ssd_entry_gradient(grad, c, cum, out):
    rows = grad.shape[0]
    total = jnp.zeros((XW, NS), F32)
    for base in range(0, rows, SBLK):
        at = pl.ds(base, SBLK)
        scaled = grad[at, :XW].astype(F32) * spread(jnp.exp(cum[at, :]), SBLK)
        total = total + tn(scaled.astype(BF16), c[at, :])
    out[pl.ds(0, XW), :] = total
    out[pl.ds(XW, 8), :] = jnp.broadcast_to(cum[rows - 1 : rows, :], (8, 128))


def ssd_entry_gradient_call(grad, c, cum):
    return pl.pallas_call(
        ssd_entry_gradient,
        out_shape=jax.ShapeDtypeStruct((XW + 8, NS), F32),
        compiler_params=pltpu.CompilerParams(vmem_limit_bytes=VMEM_LIMIT),
        name="ssd_entry_gradient",
    )(grad, c, cum)


def ssd_backward(
    slab, halo, taps, par, grad, entry, cum_all, entering, near, mid, far,
    grad_in, grad_dt, grad_rim, grad_taps, grad_par, ext, gpre,
):
    length = slab.shape[0]
    chunks = length // SBLK
    ext[pl.ds(0, HALO), :] = halo[...].astype(F32)
    ext[pl.ds(HALO, length), :] = slab[:, :CW].astype(F32)
    gpre[pl.ds(length, HALO), :] = jnp.zeros((HALO, CW), F32)
    weights = taps[...]
    lower = iota((SBLK, SBLK), 0) >= iota((SBLK, SBLK), 1)
    tri = lower.astype(F32)
    upper = (iota((SBLK, SBLK), 0) <= iota((SBLK, SBLK), 1)).astype(F32)
    hsum = head_sum_matrix()
    rate = jnp.exp(par[0:1, :])
    skip = spread(par[2:3, :], 1)
    enter = entering[...]
    later = near[pl.ds(0, XW), :] + shrink_rows(near[XW : XW + 1, :]) * (
        mid[pl.ds(0, XW), :] + shrink_rows(mid[XW : XW + 1, :]) * far[pl.ds(0, XW), :]
    )
    g_decay = jnp.zeros((1, 128), F32)
    g_bias = jnp.zeros((1, 128), F32)
    g_skip = jnp.zeros((1, 128), F32)
    for k in reversed(range(chunks)):
        base = k * SBLK
        at = pl.ds(base, SBLK)
        pre = conv_pre(ext, weights, base)
        sig = jax.nn.sigmoid(pre)
        conv = pre * sig
        b_low = conv[:, :NS].astype(BF16)
        c_low = conv[:, NS : 2 * NS].astype(BF16)
        x = conv[:, 2 * NS :]
        raw, step, log = step_and_log(slab, par, base)
        cum = nn(tri, log, HIGHEST)
        cum_t = cum.T
        last = cum[SBLK - 1 : SBLK, :]
        step_wide = spread(step, SBLK)
        u_low = (x * step_wide).astype(BF16)
        u = u_low.astype(F32)
        gy_low = grad[at, :XW]
        gy = gy_low.astype(F32)
        if k:
            state = entry[k] + shrink_rows(cum_all[base - 1 : base, :]) * enter
        else:
            state = enter
        state_low = state.astype(BF16)
        later_low = later.astype(BF16)
        inner = nt(c_low, b_low)
        g_inner = jnp.zeros((SBLK, SBLK), F32)
        y_parts, gu_parts = [], []
        for h in range(XW // HP):
            lanes = slice(h * HP, (h + 1) * HP)
            decay = jnp.exp(
                jnp.where(lower, cum[:, h : h + 1] - cum_t[h : h + 1, :], MASKED)
            )
            kernel = (inner * decay).astype(BF16)
            y_parts.append(nn(kernel, u_low[:, lanes]))
            gu_parts.append(tn(kernel, gy_low[:, lanes]))
            g_inner = g_inner + nt(gy_low[:, lanes], u_low[:, lanes]) * decay
        g_inner_low = g_inner.astype(BF16)
        enter_wide = spread(jnp.exp(cum), SBLK)
        tail_wide = spread(jnp.exp(last - cum), SBLK)
        gy_scaled = (gy * enter_wide).astype(BF16)
        u_scaled = (u * tail_wide).astype(BF16)
        y = jnp.concatenate(y_parts, axis=1) + nt(c_low, state_low) * enter_wide
        tail = nt(b_low, later_low) * tail_wide
        gu = jnp.concatenate(gu_parts, axis=1) + tail
        gc = nn(g_inner_low, b_low) + nn(gy_scaled, state_low)
        gb = tn(g_inner_low, c_low) + nn(u_scaled, later_low)
        shrink = shrink_rows(last)
        both = nn(gy * y - u * gu, hsum, HIGHEST)
        tail_sum = jnp.sum(nn(u * tail, hsum, HIGHEST), axis=0, keepdims=True)
        across = jnp.sum(
            jnp.sum(later * state * shrink, axis=1, keepdims=True) * hsum, axis=0, keepdims=True
        )
        g_log = nn(upper, both, HIGHEST) + tail_sum + across
        g_step = nn(x * gu, hsum, HIGHEST) - rate * g_log
        g_raw = g_step * jax.nn.sigmoid(raw)
        g_decay = g_decay + jnp.sum(g_log * log, axis=0, keepdims=True)
        g_bias = g_bias + jnp.sum(g_raw, axis=0, keepdims=True)
        g_skip = g_skip + jnp.sum(nn(gy * x, hsum, HIGHEST), axis=0, keepdims=True)
        grad_dt[at, :] = g_raw
        g_conv = jnp.concatenate([gb, gc, step_wide * gu + skip * gy], axis=1)
        gpre[at, :] = g_conv * (sig + conv * (1.0 - sig))
        later = shrink * later + tn(gy_scaled, c_low)
    for k in range(chunks):
        base = k * SBLK
        acc = gpre[pl.ds(base + 3, SBLK), :] * weights[0:1, :]
        for tap in range(1, KW):
            acc = acc + gpre[pl.ds(base + 3 - tap, SBLK), :] * weights[tap : tap + 1, :]
        grad_in[pl.ds(base, SBLK), :] = acc
    first = gpre[pl.ds(0, 8), :]
    rim = jnp.zeros((8, CW), F32)
    rows = iota((8, CW), 0)
    for back in range(1, KW):
        term = jnp.zeros((1, CW), F32)
        for tap in range(KW):
            t = 3 - tap - back
            if 0 <= t:
                term = term + first[t : t + 1, :] * weights[tap : tap + 1, :]
        rim = jnp.where(rows == 8 - back, term, rim)
    grad_rim[...] = rim
    g_taps = jnp.zeros((8, CW), F32)
    rows = iota((8, CW), 0)
    for tap in range(KW):
        total = jnp.zeros((1, CW), F32)
        for k in range(chunks):
            base = k * SBLK
            total = total + jnp.sum(
                gpre[pl.ds(base, SBLK), :] * ext[pl.ds(base + HALO - 3 + tap, SBLK), :],
                axis=0,
                keepdims=True,
            )
        g_taps = jnp.where(rows == tap, total, g_taps)
    grad_taps[...] = g_taps
    rows = iota((8, 128), 0)
    grad_par[...] = jnp.where(
        rows == 0, g_decay, jnp.where(rows == 1, g_bias, jnp.where(rows == 2, g_skip, 0.0))
    )


def ssd_backward_call(slab, halo, taps, par, grad, entry, cum, entering, near, mid, far):
    length = slab.shape[0]
    return pl.pallas_call(
        ssd_backward,
        out_shape=(
            jax.ShapeDtypeStruct((length, CW), F32),
            jax.ShapeDtypeStruct((length, 128), F32),
            jax.ShapeDtypeStruct((8, CW), F32),
            jax.ShapeDtypeStruct((8, CW), F32),
            jax.ShapeDtypeStruct((8, 128), F32),
        ),
        scratch_shapes=[
            pltpu.VMEM((length + HALO, CW), F32),
            pltpu.VMEM((length + HALO, CW), F32),
        ],
        compiler_params=pltpu.CompilerParams(vmem_limit_bytes=VMEM_LIMIT),
        cost_estimate=pl.CostEstimate(
            flops=20_000_000_000, bytes_accessed=12_000_000, transcendentals=2_000_000
        ),
        name="ssd_backward",
    )(slab, halo, taps, par, grad, entry, cum, entering, near, mid, far)


QB = 256
KB = 512


def place_keys(rank, parts, kv):
    length = parts[0].shape[0]
    for back, part in enumerate(parts):

        @pl.when(rank >= back)
        def _():
            kv[pl.ds(pl.multiple_of((rank - back) * length, length), length), :] = part[...]


def attend_forward(rank_ref, slab, near, mid, far, out, lse, kv, own):
    length = slab.shape[0]
    rank = rank_ref[0]
    offset = rank * length
    scale = HP**-0.5
    ahead = iota((QB, KB), 0) - iota((QB, KB), 1)
    own[...] = slab[:, KV_AT:DT_AT]
    place_keys(rank, (own, near, mid, far), kv)

    def q_step(i, _):
        at = pl.ds(pl.multiple_of(i * QB, QB), QB)
        q_blk = (slab[at, Q_AT:KV_AT].astype(F32) * scale).astype(BF16)
        first = offset + i * QB

        def block(j, carry, masked):
            top, total, acc = carry
            at = pl.ds(pl.multiple_of(j * KB, KB), KB)
            s = nt(q_blk, kv[at, :HP])
            if masked:
                s = jnp.where(ahead >= j * KB - first, s, MASKED)
            new = jnp.maximum(top, jnp.max(s, axis=1, keepdims=True))
            p = jnp.exp(s - new)
            fade = jnp.exp(top - new)
            total = total * fade + jnp.sum(p, axis=1, keepdims=True)
            acc = acc * fade + nn(p.astype(BF16), kv[at, HP:])
            return new, total, acc

        whole = first // KB
        carry = (
            jnp.full((QB, 1), MASKED, F32),
            jnp.zeros((QB, 1), F32),
            jnp.zeros((QB, HP), F32),
        )
        carry = lax.fori_loop(0, whole, lambda j, c: block(j, c, False), carry)
        top, total, acc = block(whole, carry, True)
        out[at, :] = acc / total
        lse[at, :] = jnp.broadcast_to(top + jnp.log(total), (QB, 128))
        return 0

    lax.fori_loop(0, length // QB, q_step, 0)


def attend_forward_call(rank, slab, near, mid, far):
    length = slab.shape[0]
    vm = pl.BlockSpec(memory_space=pltpu.VMEM)
    return pl.pallas_call(
        attend_forward,
        in_specs=[pl.BlockSpec(memory_space=pltpu.SMEM)] + [vm] * 4,
        out_shape=(
            jax.ShapeDtypeStruct((length, HP), F32),
            jax.ShapeDtypeStruct((length, 128), F32),
        ),
        scratch_shapes=[
            pltpu.VMEM((4 * length, 2 * HP), BF16),
            pltpu.VMEM((length, 2 * HP), BF16),
        ],
        compiler_params=pltpu.CompilerParams(vmem_limit_bytes=VMEM_LIMIT),
        cost_estimate=pl.CostEstimate(
            flops=8_000_000_000, bytes_accessed=4_000_000, transcendentals=4_000_000
        ),
        name="attend_forward",
    )(rank, slab, near, mid, far)


def attend_backward(
    rank_ref, slab, near, mid, far, g, out, lse, gq, g_own, g_near, g_mid, g_far, kv, own, acc
):
    length = slab.shape[0]
    rank = rank_ref[0]
    offset = rank * length
    scale = HP**-0.5
    ahead = iota((QB, KB), 0) - iota((QB, KB), 1)
    own[...] = slab[:, KV_AT:DT_AT]
    place_keys(rank, (own, near, mid, far), kv)
    acc[...] = jnp.zeros_like(acc)

    def q_step(i, _):
        at_q = pl.ds(pl.multiple_of(i * QB, QB), QB)
        q_blk = (slab[at_q, Q_AT:KV_AT].astype(F32) * scale).astype(BF16)
        g_low = g[at_q, XW:]
        delta = jnp.sum(g_low.astype(F32) * out[at_q, :], axis=1, keepdims=True)
        log_total = lse[at_q, 0:1]
        first = offset + i * QB

        def block(j, gq_acc, masked):
            at = pl.ds(pl.multiple_of(j * KB, KB), KB)
            k_blk = kv[at, :HP]
            s = nt(q_blk, k_blk)
            if masked:
                s = jnp.where(ahead >= j * KB - first, s, MASKED)
            p = jnp.exp(s - log_total)
            dp = nt(g_low, kv[at, HP:])
            ds = (p * (dp - delta)).astype(BF16)
            acc[at, :] += jnp.concatenate([tn(ds, q_blk), tn(p.astype(BF16), g_low)], axis=1)
            return gq_acc + nn(ds, k_blk)

        whole = first // KB
        carry = jnp.zeros((QB, HP), F32)
        carry = lax.fori_loop(0, whole, lambda j, c: block(j, c, False), carry)
        gq[at_q, :] = block(whole, carry, True) * scale
        return 0

    lax.fori_loop(0, length // QB, q_step, 0)
    for back, target in enumerate((g_own, g_near, g_mid, g_far)):

        @pl.when(rank >= back)
        def _():
            at = pl.ds(pl.multiple_of((rank - back) * length, length), length)
            target[...] = acc[at, :].astype(target.dtype)

        @pl.when(rank < back)
        def _():
            target[...] = jnp.zeros_like(target)


def attend_backward_call(rank, slab, near, mid, far, g, out, lse):
    length = slab.shape[0]
    vm = pl.BlockSpec(memory_space=pltpu.VMEM)
    keys = jax.ShapeDtypeStruct((length, 2 * HP), BF16)
    return pl.pallas_call(
        attend_backward,
        in_specs=[pl.BlockSpec(memory_space=pltpu.SMEM)] + [vm] * 7,
        out_shape=(
            jax.ShapeDtypeStruct((length, HP), F32),
            jax.ShapeDtypeStruct((length, 2 * HP), F32),
            keys,
            keys,
            keys,
        ),
        scratch_shapes=[
            pltpu.VMEM((4 * length, 2 * HP), BF16),
            pltpu.VMEM((length, 2 * HP), BF16),
            pltpu.VMEM((4 * length, 2 * HP), F32),
        ],
        compiler_params=pltpu.CompilerParams(vmem_limit_bytes=VMEM_LIMIT),
        cost_estimate=pl.CostEstimate(
            flops=20_000_000_000, bytes_accessed=4_000_000, transcendentals=4_000_000
        ),
        name="attend_backward",
    )(rank, slab, near, mid, far, g, out, lse)


HM = 24
GROUPS = 8
HEADS = 8
KEY_HEADS = 2
FF = 2048
DS = 1536
PROJ = 4120
PROJ_WIDE = 4352
EPSILON = 1e-05
TOKEN_AXES = ("fs", "cp", "ux", "uc")


def rms_norm(values, norm_gain):
    return (
        values * lax.rsqrt(jnp.mean(values * values, axis=-1, keepdims=True) + EPSILON) * norm_gain
    )


def gated_norm(mixed_heads, gate_pre, norm_gain):
    return rms_norm(mixed_heads * jax.nn.silu(gate_pre), norm_gain)


def from_behind(block, distance):
    return lax.ppermute(block, "cp", [(i - distance, i) for i in range(distance, 4)])


def from_ahead(block, distance):
    return lax.ppermute(block, "cp", [(i, i - distance) for i in range(distance, 4)])


def other_core(block):
    return lax.ppermute(block, "uc", [(0, 1), (1, 0)])


def columns_half(block, half):
    width = block.shape[1] // 2
    return lax.dynamic_slice_in_dim(block, half * width, width, 1)


def weight_gradient(left, right, core):
    lefts = jnp.concatenate([left, other_core(left)], axis=0)
    rights = jnp.concatenate(
        [columns_half(right, core), other_core(columns_half(right, 1 - core))], axis=0
    )
    part = tn(lefts, rights).astype(BF16)
    for axis in ("fs", "cp", "ux"):
        part = lax.psum_scatter(part, axis, scatter_dimension=0, tiled=True)
    rows = part.shape[0] // 2
    mine = lax.dynamic_slice_in_dim(part, core * rows, rows, 0)
    theirs = other_core(lax.dynamic_slice_in_dim(part, (1 - core) * rows, rows, 0))
    return jnp.concatenate(
        [jnp.where(core == 0, mine, theirs), jnp.where(core == 0, theirs, mine)], axis=1
    ).astype(F32)


def shards(
    tokens,
    norm_in,
    norm_mid,
    mamba_gain,
    conv_weight,
    decay_log,
    dt_bias,
    skip_gain,
    w_in,
    w_mout,
    w_aout,
    w_gu,
    w_down,
    grad_out,
):
    part_rank = lax.axis_index("cp")
    core = lax.axis_index("uc")
    group = lax.axis_index("ux") * 2 + core
    rows = tokens.shape[0]
    length = GROUPS * rows
    heads = HM // GROUPS
    full_in, full_mout, full_aout, full_gu, full_down = (
        lax.all_gather(w, "fs", axis=0, tiled=True) for w in (w_in, w_mout, w_aout, w_gu, w_down)
    )

    def to_groups(blocks):
        return lax.all_to_all(blocks, ("ux", "uc"), split_axis=0, concat_axis=0, tiled=True)

    resid_in = tokens.astype(F32)
    normed_f, in_back = jax.vjp(rms_norm, resid_in, norm_in)
    normed_in = normed_f.astype(BF16)
    projected = nn(normed_in, full_in)
    gate_pre = projected[:, :DS]
    low = projected[:, DS:].astype(BF16)
    q_at = DS + 2 * NS + HM
    k_at = q_at + HEADS * HP
    v_at = k_at + KEY_HEADS * HP
    blocks = []
    for g in range(GROUPS):
        key = g * KEY_HEADS // GROUPS
        blocks.append(
            jnp.concatenate(
                [
                    low[:, DS : DS + 2 * NS],
                    low[:, g * XW : (g + 1) * XW],
                    low[:, q_at + g * HP : q_at + (g + 1) * HP],
                    low[:, k_at + key * HP : k_at + (key + 1) * HP],
                    low[:, v_at + key * HP : v_at + (key + 1) * HP],
                    low[:, DS + 2 * NS + g * heads : DS + 2 * NS + (g + 1) * heads],
                    jnp.zeros((rows, 128 - heads), BF16),
                ],
                axis=1,
            )
        )
    slab = to_groups(jnp.stack(blocks)).reshape(length, DT_AT + 128)

    taps = jnp.concatenate(
        [conv_weight[:, DS:], lax.dynamic_slice_in_dim(conv_weight, group * XW, XW, 1)], axis=1
    )
    taps = jnp.pad(taps, ((0, 8 - KW), (0, 0)))
    per_head = jnp.stack([decay_log, dt_bias, skip_gain])
    par = jnp.pad(
        lax.dynamic_slice_in_dim(per_head, group * heads, heads, 1), ((0, 5), (0, 128 - heads))
    )
    rank = part_rank.astype(jnp.int32).reshape(1)

    halo = from_behind(slab[length - HALO :, :CW], 1)
    own_keys = slab[:, KV_AT:DT_AT]
    keys = [from_behind(own_keys, d) for d in (1, 2, 3)]
    y, state, c_low, cum, entry = ssd_forward_call(slab, halo, taps, par)
    states = [from_behind(state, d) for d in (1, 2, 3)]
    attended, lse = attend_forward_call(rank, slab, *keys)
    joined, entering = ssd_join_call(y, c_low, cum, *states, attended)
    tok = to_groups(joined.reshape(GROUPS, rows, XW + HP)).transpose(1, 0, 2)
    mixed_tok = tok[:, :, :XW].reshape(rows, DS)
    attended_tok = tok[:, :, XW:].reshape(rows, HEADS * HP)

    branch_f, gate_back = jax.vjp(gated_norm, mixed_tok.astype(F32), gate_pre, mamba_gain)
    branch_low = branch_f.astype(BF16)
    resid_mid = resid_in + nn(branch_low, full_mout) + nn(attended_tok, full_aout)
    normed_mid_f, mid_back = jax.vjp(rms_norm, resid_mid, norm_mid)
    normed_mid = normed_mid_f.astype(BF16)
    gate_up = nn(normed_mid, full_gu)
    gate_half = gate_up[:, :FF]
    up_half = gate_up[:, FF:]
    sigmoid_gate = jax.nn.sigmoid(gate_half)
    hidden = (gate_half * sigmoid_gate * up_half).astype(BF16)
    layer_out = (resid_mid + nn(hidden, full_down)).astype(BF16)
    grad_hidden = nt(grad_out, full_down)
    grad_gate = grad_hidden * up_half * sigmoid_gate * (1.0 + gate_half * (1.0 - sigmoid_gate))
    grad_up = grad_hidden * gate_half * sigmoid_gate
    grad_gate_up = jnp.concatenate([grad_gate, grad_up], axis=1).astype(BF16)
    resid_back, grad_norm_mid = mid_back(nt(grad_gate_up, full_gu))
    grad_resid = grad_out.astype(F32) + resid_back
    resid_low = grad_resid.astype(BF16)
    grad_mixed, grad_gate_pre, grad_mamba_gain = gate_back(nt(resid_low, full_mout))
    grad_attended = nt(resid_low, full_aout)
    grad_blocks = jnp.concatenate(
        [
            grad_mixed.astype(BF16).reshape(rows, GROUPS, XW),
            grad_attended.astype(BF16).reshape(rows, GROUPS, HP),
        ],
        axis=2,
    ).transpose(1, 0, 2)
    grad = to_groups(grad_blocks).reshape(length, XW + HP)
    grad_down = weight_gradient(hidden, grad_out, core)
    grad_gu = weight_gradient(normed_mid, grad_gate_up, core)
    grad_mout = weight_gradient(branch_low, resid_low, core)
    grad_aout = weight_gradient(attended_tok, resid_low, core)

    entry_gradient = ssd_entry_gradient_call(grad, c_low, cum)
    later = [from_ahead(entry_gradient, d) for d in (1, 2, 3)]
    grad_query, key_own, *key_parts = attend_backward_call(rank, slab, *keys, grad, attended, lse)
    key_parts = [from_ahead(p, d + 1) for d, p in enumerate(key_parts)]
    grad_in_cols, grad_dt, rim, grad_taps, grad_par = ssd_backward_call(
        slab, halo, taps, par, grad, entry, cum, entering, *later
    )
    rim = from_ahead(rim, 1)
    grad_cols = jnp.concatenate(
        [grad_in_cols[: length - 8], grad_in_cols[length - 8 :] + rim], axis=0
    )
    grad_keys = key_own + sum(p.astype(F32) for p in key_parts)
    back = jnp.concatenate(
        [grad_cols.astype(BF16), grad_query.astype(BF16), grad_keys.astype(BF16), grad_dt.astype(BF16)],
        axis=1,
    )
    back = to_groups(back.reshape(GROUPS, rows, DT_AT + 128))
    grad_x = back[:, :, 2 * NS : CW].transpose(1, 0, 2).reshape(rows, DS)
    grad_bc = jnp.sum(back[:, :, : 2 * NS].astype(F32), axis=0).astype(BF16)
    grad_q = back[:, :, Q_AT:KV_AT].transpose(1, 0, 2).reshape(rows, HEADS * HP)
    shared = back[:, :, KV_AT:DT_AT].astype(F32).reshape(KEY_HEADS, GROUPS // KEY_HEADS, rows, 2, HP)
    grad_kv = jnp.sum(shared, axis=1).transpose(1, 2, 0, 3).reshape(rows, 2 * KEY_HEADS * HP)
    grad_dt_tok = back[:, :, DT_AT : DT_AT + heads].transpose(1, 0, 2).reshape(rows, HM)
    grad_proj = jnp.concatenate(
        [
            grad_gate_pre.astype(BF16),
            grad_x,
            grad_bc,
            grad_dt_tok,
            grad_q,
            grad_kv.astype(BF16),
            jnp.zeros((rows, PROJ_WIDE - PROJ), BF16),
        ],
        axis=1,
    )
    grad_in = weight_gradient(normed_in, grad_proj, core)[:, :PROJ]
    tokens_back, grad_norm_in = in_back(nt(grad_proj[:, :PROJ], full_in))
    grad_tokens = grad_resid + tokens_back

    conv_full = jnp.concatenate(
        [
            lax.dynamic_update_slice_in_dim(
                jnp.zeros((KW, DS), F32), grad_taps[:KW, 2 * NS :], group * XW, 1
            ),
            grad_taps[:KW, : 2 * NS],
        ],
        axis=1,
    )
    head_full = lax.dynamic_update_slice_in_dim(
        jnp.zeros((3, HM), F32), grad_par[:3, :heads], group * heads, 1
    )
    small = lax.psum(
        (grad_norm_in, grad_norm_mid, grad_mamba_gain, conv_full, head_full), TOKEN_AXES
    )
    return (
        layer_out,
        grad_tokens,
        small[0],
        small[1],
        small[2],
        small[3],
        small[4][0],
        small[4][1],
        small[4][2],
        grad_in,
        grad_mout,
        grad_aout,
        grad_gu,
        grad_down,
    )


def solution(mesh):
    fine = Mesh(mesh.devices.reshape(4, 4, 4, 2), TOKEN_AXES)
    by_token = P(TOKEN_AXES, None)
    by_row = P("fs", None)
    return jax.shard_map(
        shards,
        mesh=fine,
        in_specs=(by_token,) + (P(),) * 7 + (by_row,) * 5 + (by_token,),
        out_specs=(by_token, by_token) + (P(),) * 7 + (by_token,) * 5,
        check_vma=False,
    )
```

time: 2320 us -> 755 us (0.33)
  waiting for transfers between devices: 1020 us -> 412 us
  blocking collectives: 564 us -> 81.8 us
  local copies, waits for them, and re-layouts: 243 us -> 47.6 us
  matrix products: 178 us -> 55.5 us
  other arithmetic: 118 us -> 20 us
  starting transfers between devices: 145 us -> 60.8 us
  Pallas kernels: 0 us -> 50.7 us
    reduce_scatter x3 -> x15, waiting for transfers between devices: 906 us -> 165 us  [weight_gradient(): part = lax.psum_scatter(part, axis, scatter_dimension=0, tiled=True)]
    unnamed x1 -> x0, blocking collectives: 382 us -> none
    dot_general x81 -> x15, matrix products: 178 us -> 55.5 us  [the longest x5 20.5 us: nt(): lax.dot_general(a, b, (((1,), (1,)), ((), ())), preferred_element_type=F32)]
    all_gather x5 -> x0, blocking collectives: 114 us -> none  [the longest x3 86.9 us: entering_2(): lax.all_gather(a.astype(kind), axis)]
    all_gather x5, waiting for transfers between devices: 88.9 us -> 184 us  [shards(): lax.all_gather(w, 'fs', axis=0, tiled=True)]
    unnamed x33 -> x0, starting transfers between devices: 93 us -> none
    dynamic_update_slice x78 -> x2, local copies, waits for them, and re-layouts: 72.6 us -> 0.58 us  [the longest x1 0.33 us: shards(): lax.dynamic_update_slice_in_dim(jnp.zeros((KW, DS), F32), grad_taps[:KW,...]
    unnamed x268 -> x133, local copies, waits for them, and re-layouts: 82.6 us -> 18.4 us
  transfers between devices with their start and end apart: 51 -> 51, of which waited for: 7 -> 24; matrix products, arithmetic and copies ran while one was open for 38% -> 14% of each run, Pallas kernels for 0% -> 7%
where the time goes in v1:
time: 755 us; the launch traced here: 744 us
  waiting for transfers between devices  412 us (55%)
  blocking collectives  81.8 us (11%)
  starting transfers between devices  60.8 us (8%)
  matrix products  55.5 us (7%)
  Pallas kernels  50.7 us (7%)
  local copies, waits for them, and re-layouts  47.6 us (6%)
  other arithmetic  20 us (3%)
  between operations  15.9 us (2%)
    all_gather x5, waiting for transfers between devices, shards(): lax.all_gather(w, 'fs', axis=0, tiled=True)  184 us
    reduce_scatter x15, waiting for transfers between devices, weight_gradient(): part = lax.psum_scatter(part, axis, scatter_dimension=0, tiled=True)  165 us
    psum x1, blocking collectives, shards(): lax.psum((grad_norm_in, grad_norm_mid, grad_mamba_gain, conv_full, head_f...  66.3 us
    all_to_all x3, waiting for transfers between devices, to_groups(): lax.all_to_all(blocks, ('ux', 'uc'), split_axis=0, concat_axis=0, tiled=T...  47.5 us
    pallas_call x1, Pallas kernels, ssd_backward_call(): pl.pallas_call(ssd_backward, out_shape=(jax.ShapeDtypeStruct((length, CW)...  22 us
    dot_general x5, matrix products, nt(): lax.dot_general(a, b, (((1,), (1,)), ((), ())), preferred_element_type=F32)  20.5 us
    dot_general x5, matrix products, nn(): lax.dot_general(a, b, (((1,), (0,)), ((), ())), precision=precision, pref...  19.7 us
    unnamed x133, local copies, waits for them, and re-layouts  18.4 us
  transfers between devices with their start and end apart: 51, of which 24 were waited for; matrix products, arithmetic and copies ran while one was open for 14% of the time, Pallas kernels for 7%

profile of v1, /device:TPU:1, one launch (start us, length us, event | category | flops | bytes accessed | tf_op | source)
XLA Modules:
  0.0 744.4 jit_solution(14227677062063748481)
XLA Ops:
  10.9 89.0 %all-gather.6.cloned.1.call-done = bf16[1024,4120]{0,1:T(8,128)(2,1)} async-done(((bf16[256,4120]{0,1:T(8,128)(2,1)}), bf16[1024,4120]{0,1:T(8,128)(2,1)}) %all-gather.6.cloned.1.call-update) | async-done | bytes 8437776 | tf_op jit(solution)/shard_map/all_gather | solution.py:567
  99.9 4.8 fusion.54
  113.3 6.0 all-to-all-start
  120.0 20.1 %all-to-all-done = bf16[8,128,768]{1,2,0:T(8,128)(2,1)} async-done(((bf16[8,128,768]{1,2,0:T(8,128)(2,1)}), bf16[8,128,768]{1,2,0:T(8,128)(2,1)}, u32[]{:S(2)}, u32[]{:S(2)}) %all-to-all-start) | async-done | bytes 1572896 | tf_op jit(solution)/shard_map/all_to_all | solution.py:571
  156.6 7.4 ssd_forward.1
  168.8 6.1 attend_forward.1
  180.8 5.0 all-to-all-start.1
  186.1 9.2 %all-to-all-done.1 = bf16[8,128,256]{1,2,0:T(8,128)(2,1)S(1)} async-done(((bf16[8,128,256]{1,2,0:T(8,128)(2,1)}), bf16[8,128,256]{1,2,0:T(8,128)(2,1)S(1)}, u32[]{:S(2)}, u32[]{:S(2)}) %all-to-all-start.1) | async-done | bytes 524320 | tf_op jit(solution)/shard_map/all_to_all | solution.py:571
  202.6 50.6 %all-gather.12.cloned.1.call-done = bf16[1024,4096]{1,0:T(8,128)(2,1)} async-done(((bf16[256,4096]{1,0:T(8,128)(2,1)}), bf16[1024,4096]{1,0:T(8,128)(2,1)}) %all-gather.12.cloned.1.call-update) | async-done | bytes 8388624 | tf_op jit(solution)/shard_map/all_gather | solution.py:567
  253.2 6.0 fusion.55
  259.2 44.8 %all-gather.14.cloned.1.call-done = bf16[2048,1024]{1,0:T(8,128)(2,1)} async-done(((bf16[512,1024]{1,0:T(8,128)(2,1)}), bf16[2048,1024]{1,0:T(8,128)(2,1)}) %all-gather.14.cloned.1.call-update) | async-done | bytes 4194320 | tf_op jit(solution)/shard_map/all_gather | solution.py:567
  304.0 5.6 multiply_convert_fusion.1
  332.5 5.8 reduce-scatter.28.cloned.1.call-done
  338.4 4.6 convolution_convert_fusion.1
  349.8 4.0 multiply_reduce_fusion
  356.8 15.6 %all_to_all.20 = bf16[8,128,256]{2,1,0:T(8,128)(2,1)} all-to-all(bf16[8,128,256]{2,1,0:T(8,128)(2,1)S(1)} %maximum_bitcast_fusion), channel_id=1, replica_groups=mesh['fs'=4,'cp'=4,'ux'=4,'uc'=2] {'ux','uc'}, dimensions={0} | all-to-all | bytes 1048576 | tf_op jit(solution)/shard_map/all_to_all | solution.py:571
  379.0 9.2 %attend_backward.1 = (f32[1024,64]{1,0:T(8,128)}, f32[1024,128]{1,0:T(8,128)}, bf16[1024,128]{1,0:T(8,128)(2,1)}, bf16[1024,128]{1,0:T(8,128)(2,1)}, bf16[1024,128]{1,0:T(8,128)(2,1)}) custom-call(s32[1]{0:T(128)} %bitcast.12.rank_ref, bf16[1024,768]{1,0:T(8,128)(2,1)} %bitcast.89, bf16[1024,128]{1,0:T(8,128)(2,1)} %copy-done.52, ...), custom_call_target="tpu_custom_call" | custom-call | flops 20000000000 | bytes 4000000 | tf_op jit(solution)/shard_map/attend_backward/pallas_call | solution.py:466
  390.9 10.0 %collective-permute-start.11 = (bf16[1024,128]{1,0:T(8,128)(2,1)}, bf16[1024,128]{1,0:T(8,128)(2,1)S(1)}, u32[]{:S(2)}, u32[]{:S(2)}) collective-permute-start(bf16[1024,128]{1,0:T(8,128)(2,1)} %get-tuple-element.46), channel_id=1, source_target_pairs={{8,0},{16,8},{24,16},{9,1},{17,9},{25,17},{10,2},{18,10},{26,18},{... | collective-permute-start | bytes 786440 | tf_op jit(solution)/shard_map/ppermute | solution.py:516
  401.6 22.0 %ssd_backward.1 = (f32[1024,448]{1,0:T(8,128)}, f32[1024,128]{1,0:T(8,128)}, f32[8,448]{1,0:T(8,128)}, f32[8,448]{1,0:T(8,128)}, f32[8,128]{1,0:T(8,128)}) custom-call(bf16[1024,768]{1,0:T(8,128)(2,1)} %bitcast.90, bf16[16,448]{1,0:T(8,128)(2,1)} %copy-done.59, f32[8,448]{1,0:T(8,128)} %select_maximum_fusion.taps, f32[8,128]{1,0:T(8,128)} %pad.9.par, ...), custom_call_target="tpu_custom_call" | custom-call | flops 20000000000 | bytes 12000000 | tf_op jit(solution)/shard_map/ssd_backward/pallas_call | solution.py:313
  429.3 5.0 collective-permute-done.10
  438.1 5.6 all-to-all-start.3
  446.2 18.2 %all-to-all-done.3 = bf16[8,128,768]{1,2,0:T(8,128)(2,1)S(1)} async-done(((bf16[8,128,768]{1,2,0:T(8,128)(2,1)}), bf16[8,128,768]{1,2,0:T(8,128)(2,1)S(1)}, u32[]{:S(2)}, u32[]{:S(2)}) %all-to-all-start.3) | async-done | bytes 1572896 | tf_op jit(solution)/shard_map/all_to_all | solution.py:571
  485.0 7.7 %reduce-scatter.24.cloned.1.call-done = bf16[96,512]{1,0:T(8,128)(2,1)} async-done(((bf16[384,512]{1,0:T(8,128)(2,1)}), bf16[96,512]{1,0:T(8,128)(2,1)}) %reduce-scatter.24.cloned.1.call-update) | async-done | bytes 98320 | tf_op jit(solution)/shard_map/reduce_scatter | solution.py:535
  492.8 23.9 %reduce-scatter.42.cloned.1.call-done = bf16[128,512]{1,0:T(8,128)(2,1)} async-done(((bf16[512,512]{1,0:T(8,128)(2,1)}), bf16[128,512]{1,0:T(8,128)(2,1)}) %reduce-scatter.42.cloned.1.call-update) | async-done | bytes 131088 | tf_op jit(solution)/shard_map/reduce_scatter | solution.py:535
  516.8 3.6 fusion
  520.8 17.5 %reduce-scatter.32.cloned.1.call-done = bf16[8,512]{1,0:T(8,128)(2,1)} async-done(((bf16[32,512]{1,0:T(8,128)(2,1)}), bf16[8,512]{1,0:T(8,128)(2,1)}) %reduce-scatter.32.cloned.1.call-update) | async-done | bytes 8208 | tf_op jit(solution)/shard_map/reduce_scatter | solution.py:535
  541.9 23.2 %reduce-scatter.36.cloned.1.call-done = bf16[64,2048]{1,0:T(8,128)(2,1)} async-done(((bf16[256,2048]{1,0:T(8,128)(2,1)}), bf16[64,2048]{1,0:T(8,128)(2,1)}) %reduce-scatter.36.cloned.1.call-update) | async-done | bytes 262160 | tf_op jit(solution)/shard_map/reduce_scatter | solution.py:535
  566.8 50.5 %reduce-scatter.16.cloned.1.call-done = bf16[256,2176]{1,0:T(8,128)(2,1)} async-done(((bf16[1024,2176]{1,0:T(8,128)(2,1)}), bf16[256,2176]{1,0:T(8,128)(2,1)}) %reduce-scatter.16.cloned.1.call-update) | async-done | bytes 1114128 | tf_op jit(solution)/shard_map/reduce_scatter | solution.py:535
  617.7 5.1 fusion.21
  622.8 66.3 %all-reduce.2 = (f32[1024]{0:T(1024)}, f32[1024]{0:T(1024)}, f32[1536]{0:T(1024)}, f32[4,1792]{1,0:T(4,128)}, f32[3,24]{1,0:T(4,128)S(1)}) all-reduce(f32[1024]{0:T(1024)S(1)} %get-tuple-element.56, f32[1024]{0:T(1024)S(1)} %copy-done.29, f32[1536]{0:T(1024)S(1)} %copy-done.31, ...), channel_id=1, replica_groups=mesh['fs'=4,'cp'=4,'ux'=4,'uc'=2] {'fs','cp','ux','uc'}, use_global_device_ids=true, to_apply=%region_9.10 | all-reduce | flops 10824 | bytes 86592 | tf_op jit(solution)/shard_map/psum | solution.py:706
  697.0 12.6 %reduce-scatter.18.cloned.1.call-done = bf16[64,2176]{1,0:T(8,128)(2,1)} async-done(((bf16[256,2176]{1,0:T(8,128)(2,1)}), bf16[64,2176]{1,0:T(8,128)(2,1)}) %reduce-scatter.18.cloned.1.call-update) | async-done | bytes 278544 | tf_op jit(solution)/shard_map/reduce_scatter | solution.py:535
  711.1 20.1 %reduce-scatter.20.cloned.1.call-done = bf16[16,2176]{1,0:T(8,128)(2,1)} async-done(((bf16[64,2176]{1,0:T(8,128)(2,1)}), bf16[16,2176]{1,0:T(8,128)(2,1)}) %reduce-scatter.20.cloned.1.call-update) | async-done | bytes 69648 | tf_op jit(solution)/shard_map/reduce_scatter | solution.py:535
  (335 shorter events, 143.4 us)
Async XLA Ops:
  7.2 92.7 %all-gather.6.cloned.1.call-start = ((), (), s32[]{:S(2)}) async-start(), calls=%async_computation.19 | async-start | bytes 10547200 | tf_op jit(solution)/shard_map/all_gather | solution.py:567
  7.9 188.1 %all-gather.8.cloned.1.call-start = ((), (), s32[]{:S(2)}) async-start(), calls=%async_computation.20 | async-start | bytes 3932160 | tf_op jit(solution)/shard_map/all_gather | solution.py:567
  8.7 190.9 %all-gather.10.cloned.1.call-start = ((), (), s32[]{:S(2)}) async-start(), calls=%async_computation.21 | async-start | bytes 1310720 | tf_op jit(solution)/shard_map/all_gather | solution.py:567
  9.4 243.8 %all-gather.12.cloned.1.call-start = ((), (), s32[]{:S(2)}) async-start(), calls=%async_computation.22 | async-start | bytes 10485760 | tf_op jit(solution)/shard_map/all_gather | solution.py:567
  10.0 294.0 %all-gather.14.cloned.1.call-start = ((), (), s32[]{:S(2)}) async-start(), calls=%async_computation.23 | async-start | bytes 5242880 | tf_op jit(solution)/shard_map/all_gather | solution.py:567
  113.3 26.8 %all-to-all-start = ((bf16[8,128,768]{1,2,0:T(8,128)(2,1)}), bf16[8,128,768]{1,2,0:T(8,128)(2,1)}, u32[]{:S(2)}, u32[]{:S(2)}) async-start(bf16[8,128,768]{1,2,0:T(8,128)(2,1)} %bitcast_dynamic-update-slice_fusion), calls=%async_computation | async-start | bytes 3145728 | tf_op jit(solution)/shard_map/all_to_all | solution.py:571
  148.3 18.4 %collective-permute-start.4 = (bf16[1024,128]{1,0:T(8,128)(2,1)S(1)}, bf16[1024,128]{1,0:T(8,128)(2,1)S(1)}, u32[]{:S(2)}, u32[]{:S(2)}) collective-permute-start(bf16[1024,128]{1,0:T(8,128)(2,1)S(1)} %slice.291), channel_id=1, source_target_pairs={{0,8},{8,16},{16,24},{1,9},{9,17},{17,25},{2,10},{10,18},{18,26},{... | collective-permute-start | bytes 786440 | tf_op jit(solution)/shard_map/ppermute | solution.py:512
  151.4 16.5 %collective-permute-start.5 = (bf16[1024,128]{1,0:T(8,128)(2,1)S(1)}, bf16[1024,128]{1,0:T(8,128)(2,1)S(1)}, u32[]{:S(2)}, u32[]{:S(2)}) collective-permute-start(bf16[1024,128]{1,0:T(8,128)(2,1)S(1)} %slice.291), channel_id=1, source_target_pairs={{0,16},{8,24},{1,17},{9,25},{2,18},{10,26},{3,19},{11,27},{4,20},{... | collective-permute-start | bytes 786440 | tf_op jit(solution)/shard_map/ppermute | solution.py:512
  180.8 14.5 %all-to-all-start.1 = ((bf16[8,128,256]{1,2,0:T(8,128)(2,1)}), bf16[8,128,256]{1,2,0:T(8,128)(2,1)S(1)}, u32[]{:S(2)}, u32[]{:S(2)}) async-start(bf16[8,128,256]{1,2,0:T(8,128)(2,1)} %copy.46), calls=%async_computation.1 | async-start | bytes 1048576 | tf_op jit(solution)/shard_map/all_to_all | solution.py:571
  185.8 152.5 %reduce-scatter.28.cloned.1.call-start = ((), (), s32[]{:S(2)}) async-start(), calls=%async_computation.30 | async-start | bytes 655360 | tf_op jit(solution)/shard_map/reduce_scatter | solution.py:535
  318.4 110.9 %reduce-scatter.22.cloned.1.call-start = ((), (), s32[]{:S(2)}) async-start(), calls=%async_computation.27 | async-start | bytes 1966080 | tf_op jit(solution)/shard_map/reduce_scatter | solution.py:535
  323.3 120.4 %reduce-scatter.40.cloned.1.call-start = ((), (), s32[]{:S(2)}) async-start(), calls=%async_computation.36 | async-start | bytes 2621440 | tf_op jit(solution)/shard_map/reduce_scatter | solution.py:535
  329.3 116.8 %reduce-scatter.30.cloned.1.call-start = ((), (), s32[]{:S(2)}) async-start(), calls=%async_computation.31 | async-start | bytes 163840 | tf_op jit(solution)/shard_map/reduce_scatter | solution.py:535
  338.3 133.1 %reduce-scatter.34.cloned.1.call-start = ((), (), s32[]{:S(2)}) async-start(), calls=%async_computation.33 | async-start | bytes 5242880 | tf_op jit(solution)/shard_map/reduce_scatter | solution.py:535
  343.1 149.6 %reduce-scatter.24.cloned.1.call-start = ((), (), s32[]{:S(2)}) async-start(), calls=%async_computation.28 | async-start | bytes 491520 | tf_op jit(solution)/shard_map/reduce_scatter | solution.py:535
  375.1 15.7 %collective-permute-start.7 = (f32[200,128]{1,0:T(8,128)}, f32[200,128]{1,0:T(8,128)S(1)}, u32[]{:S(2)}, u32[]{:S(2)}) collective-permute-start(f32[200,128]{1,0:T(8,128)} %ssd_entry_gradient.1), channel_id=1, source_target_pairs={{8,0},{16,8},{24,16},{9,1},{17,9},{25,17},{10,2},{18,10},{26,18},{... | collective-permute-start | bytes 307208 | tf_op jit(solution)/shard_map/ppermute | solution.py:516
  376.4 24.5 %collective-permute-start.8 = (f32[200,128]{1,0:T(8,128)}, f32[200,128]{1,0:T(8,128)S(1)}, u32[]{:S(2)}, u32[]{:S(2)}) collective-permute-start(f32[200,128]{1,0:T(8,128)} %ssd_entry_gradient.1), channel_id=1, source_target_pairs={{16,0},{24,8},{17,1},{25,9},{18,2},{26,10},{19,3},{27,11},{20,4},{... | collective-permute-start | bytes 307208 | tf_op jit(solution)/shard_map/ppermute | solution.py:516
  377.7 23.2 %collective-permute-start.9 = (f32[200,128]{1,0:T(8,128)}, f32[200,128]{1,0:T(8,128)S(1)}, u32[]{:S(2)}, u32[]{:S(2)}) collective-permute-start(f32[200,128]{1,0:T(8,128)} %ssd_entry_gradient.1), channel_id=1, source_target_pairs={{24,0},{25,1},{26,2},{27,3},{28,4},{29,5},{30,6},{31,7},{56,32},{5... | collective-permute-start | bytes 307208 | tf_op jit(solution)/shard_map/ppermute | solution.py:516
  388.2 46.7 %collective-permute-start.13 = (bf16[1024,128]{1,0:T(8,128)(2,1)}, bf16[1024,128]{1,0:T(8,128)(2,1)S(1)}, u32[]{:S(2)}, u32[]{:S(2)}) collective-permute-start(bf16[1024,128]{1,0:T(8,128)(2,1)} %get-tuple-element.48), channel_id=1, source_target_pairs={{24,0},{25,1},{26,2},{27,3},{28,4},{29,5},{30,6},{31,7},{56,32},{5... | collective-permute-start | bytes 786440 | tf_op jit(solution)/shard_map/ppermute | solution.py:516
  389.5 45.5 %collective-permute-start.12 = (bf16[1024,128]{1,0:T(8,128)(2,1)}, bf16[1024,128]{1,0:T(8,128)(2,1)S(1)}, u32[]{:S(2)}, u32[]{:S(2)}) collective-permute-start(bf16[1024,128]{1,0:T(8,128)(2,1)} %get-tuple-element.47), channel_id=1, source_target_pairs={{16,0},{24,8},{17,1},{25,9},{18,2},{26,10},{19,3},{27,11},{20,4},{... | collective-permute-start | bytes 786440 | tf_op jit(solution)/shard_map/ppermute | solution.py:516
  390.9 44.1 %collective-permute-start.11 = (bf16[1024,128]{1,0:T(8,128)(2,1)}, bf16[1024,128]{1,0:T(8,128)(2,1)S(1)}, u32[]{:S(2)}, u32[]{:S(2)}) collective-permute-start(bf16[1024,128]{1,0:T(8,128)(2,1)} %get-tuple-element.46), channel_id=1, source_target_pairs={{8,0},{16,8},{24,16},{9,1},{17,9},{25,17},{10,2},{18,10},{26,18},{... | collective-permute-start | bytes 786440 | tf_op jit(solution)/shard_map/ppermute | solution.py:516
  438.1 26.4 %all-to-all-start.3 = ((bf16[8,128,768]{1,2,0:T(8,128)(2,1)}), bf16[8,128,768]{1,2,0:T(8,128)(2,1)S(1)}, u32[]{:S(2)}, u32[]{:S(2)}) async-start(bf16[8,128,768]{1,2,0:T(8,128)(2,1)} %copy.51), calls=%async_computation.3 | async-start | bytes 3145728 | tf_op jit(solution)/shard_map/all_to_all | solution.py:571
  443.7 72.9 %reduce-scatter.42.cloned.1.call-start = ((), (), s32[]{:S(2)}) async-start(), calls=%async_computation.37 | async-start | bytes 655360 | tf_op jit(solution)/shard_map/reduce_scatter | solution.py:535
  444.3 94.0 %reduce-scatter.32.cloned.1.call-start = ((), (), s32[]{:S(2)}) async-start(), calls=%async_computation.32 | async-start | bytes 40960 | tf_op jit(solution)/shard_map/reduce_scatter | solution.py:535
  446.2 118.9 %reduce-scatter.36.cloned.1.call-start = ((), (), s32[]{:S(2)}) async-start(), calls=%async_computation.34 | async-start | bytes 1310720 | tf_op jit(solution)/shard_map/reduce_scatter | solution.py:535
  471.5 145.8 %reduce-scatter.16.cloned.1.call-start = ((), (), s32[]{:S(2)}) async-start(), calls=%async_computation.24 | async-start | bytes 5570560 | tf_op jit(solution)/shard_map/reduce_scatter | solution.py:535
  485.0 205.3 %reduce-scatter.26.cloned.1.call-start = ((), (), s32[]{:S(2)}) async-start(), calls=%async_computation.29 | async-start | bytes 122880 | tf_op jit(solution)/shard_map/reduce_scatter | solution.py:535
  492.7 200.5 %reduce-scatter.44.cloned.1.call-start = ((), (), s32[]{:S(2)}) async-start(), calls=%async_computation.38 | async-start | bytes 163840 | tf_op jit(solution)/shard_map/reduce_scatter | solution.py:535
  516.7 179.2 %reduce-scatter.38.cloned.1.call-start = ((), (), s32[]{:S(2)}) async-start(), calls=%async_computation.35 | async-start | bytes 327680 | tf_op jit(solution)/shard_map/reduce_scatter | solution.py:535
  539.0 26.5 %collective-permute-start.21 = (bf16[4,512]{1,0:T(4,128)(2,1)S(1)}, bf16[4,512]{1,0:T(4,128)(2,1)S(1)}, u32[]{:S(2)}, u32[]{:S(2)}) collective-permute-start(bf16[4,512]{1,0:T(4,128)(2,1)S(1)} %constant_dynamic-slice_fusion.4), channel_id=1, source_target_pairs={{0,1},{1,0},{2,3},{3,2},{4,5},{5,4},{6,7},{7,6},{8,9},{9,8},{10,11... | collective-permute-start | bytes 12296 | tf_op jit(solution)/shard_map/ppermute | solution.py:520
  565.1 144.5 %reduce-scatter.18.cloned.1.call-start = ((), (), s32[]{:S(2)}) async-start(), calls=%async_computation.25 | async-start | bytes 1392640 | tf_op jit(solution)/shard_map/reduce_scatter | solution.py:535
  617.3 113.8 %reduce-scatter.20.cloned.1.call-start = ((), (), s32[]{:S(2)}) async-start(), calls=%async_computation.26 | async-start | bytes 348160 | tf_op jit(solution)/shard_map/reduce_scatter | solution.py:535
  (80 other events, 1226.3 us)
Sparse Core Ops, SparseCore 0:
  9.7 90.1 all-gather.5
  101.5 40.7 all-gather.7
  144.0 23.2 all-gather.9
  168.8 84.3 all-gather.11
  254.7 49.2 all-gather.13
  318.5 19.7 reduce-scatter.27
  340.7 26.0 reduce-scatter.21
  369.2 30.4 reduce-scatter.39
  402.2 18.3 reduce-scatter.29
  422.9 48.5 reduce-scatter.33
  474.0 18.6 reduce-scatter.23
  494.9 21.6 reduce-scatter.41
  519.0 19.2 reduce-scatter.31
  540.6 24.3 reduce-scatter.35
  567.3 49.9 reduce-scatter.15
  619.5 17.9 reduce-scatter.25
  639.8 20.0 reduce-scatter.43
  662.1 20.4 reduce-scatter.37
  685.1 24.4 reduce-scatter.17
  711.9 19.2 reduce-scatter.19

commit v2 on v1

--- a/solution.py
+++ b/solution.py
@@ -1,4 +1,5 @@
-import functools
+import math
+
 import jax
 import jax.numpy as jnp
 from jax import lax
@@ -486,6 +487,196 @@
     )(rank, slab, near, mid, far, g, out, lse)
 
 
+CORE_ROWS = 16
+PARTS = (0, 768, 1536, 2176)
+ORDERS = ((0, 1, 2), (1, 2, 0), (2, 0, 1))
+TORUS = ("fs", "cp", "ux")
+
+
+def sum_over_devices(
+    left, right, small, out, small_out,
+    left_in, right_in, part0, part1, part2, got10, got11, got12, mid0, mid1, mid2,
+    got20, got21, got22, end0, end1, end2, got30, got31, got32, done, done_in, small_in, small_core,
+    core_send, core_recv, send, recv, small_send, small_recv,
+):
+    mesh_kind = pl.DeviceIdType.MESH
+    core = lax.axis_index("uc")
+    place = [lax.axis_index(a) for a in TORUS]
+    other = {"uc": 1 - core}
+    half = right.shape[1] // 2
+    rows = left.shape[0]
+
+    def peer(axis, shift):
+        return {TORUS[axis]: lax.rem(place[axis] + shift, 4)}
+
+    barrier = pltpu.get_barrier_semaphore()
+    pl.semaphore_signal(barrier, inc=1, device_id=other, device_id_type=mesh_kind)
+    for axis in range(3):
+        for shift in (1, 2, 3):
+            pl.semaphore_signal(
+                barrier, inc=1, device_id=peer(axis, shift), device_id_type=mesh_kind
+            )
+    pl.semaphore_wait(barrier, 10)
+
+    def remote(src, dst, send_sem, recv_sem, target):
+        copy = pltpu.make_async_remote_copy(
+            src_ref=src, dst_ref=dst, send_sem=send_sem, recv_sem=recv_sem,
+            device_id=target, device_id_type=mesh_kind,
+        )
+        copy.start()
+        return copy
+
+    theirs = pl.ds(pl.multiple_of((1 - core) * half, 128), half)
+    ours = pl.ds(pl.multiple_of(core * half, 128), half)
+    core_copies = [
+        remote(left, left_in, core_send.at[0], core_recv.at[0], other),
+        remote(right.at[:, theirs], right_in, core_send.at[1], core_recv.at[1], other),
+        remote(small, small_core, core_send.at[2], core_recv.at[2], other),
+    ]
+    for copy in core_copies:
+        copy.wait()
+
+    parts = (part0, part1, part2)
+    got1, got2, got3 = (got10, got11, got12), (got20, got21, got22), (got30, got31, got32)
+    mids, ends = (mid0, mid1, mid2), (end0, end1, end2)
+    lefts = [(left[:, f * 256 : (f + 1) * 256], left_in[:, f * 256 : (f + 1) * 256]) for f in range(4)]
+    first = []
+    for p in range(3):
+        width = PARTS[p + 1] - PARTS[p]
+        at = pl.ds(pl.multiple_of(core * half + PARTS[p], 128), width)
+        mine, their = right[:, at], right_in[:, PARTS[p] : PARTS[p + 1]]
+        rights = jnp.concatenate([mine, their], axis=0)
+        for f in range(4):
+            block = tn(jnp.concatenate(lefts[f], axis=0), rights).astype(BF16)
+            for c in range(4):
+                for x in range(4):
+                    where = (f, c, x)
+                    a0, a1, a2 = (where[a] for a in ORDERS[p])
+                    start = (c * 4 + x) * CORE_ROWS
+                    parts[p][a0, a1, a2] = block[start : start + CORE_ROWS]
+        axis = ORDERS[p][0]
+        first.append(
+            [
+                remote(
+                    parts[p].at[lax.rem(place[axis] + shift, 4)], got1[p].at[shift - 1],
+                    send.at[p, 0, shift - 1], recv.at[p, 0, shift - 1], peer(axis, shift),
+                )
+                for shift in (1, 2, 3)
+            ]
+        )
+
+    total = small[...] + small_core[...]
+    for axis in range(3):
+        small_in[axis, place[axis]] = total
+        copies = [
+            remote(
+                small_in.at[axis, place[axis]], small_in.at[axis, place[axis]],
+                small_send.at[axis, shift - 1], small_recv.at[axis, shift - 1], peer(axis, shift),
+            )
+            for shift in (1, 2, 3)
+        ]
+        for copy in copies:
+            copy.wait()
+        total = (small_in[axis, 0] + small_in[axis, 1]) + (small_in[axis, 2] + small_in[axis, 3])
+    small_out[...] = total
+
+    def add(source, slots, index):
+        acc = source[index].astype(F32)
+        for s in range(3):
+            acc = acc + slots[s].astype(F32)
+        return acc
+
+    second = []
+    for p in range(3):
+        for copy in first[p]:
+            copy.wait()
+        for i in range(4):
+            acc = parts[p][place[ORDERS[p][0]], i].astype(F32)
+            for s in range(3):
+                acc = acc + got1[p][s, i].astype(F32)
+            mids[p][i] = acc.astype(BF16)
+        axis = ORDERS[p][1]
+        second.append(
+            [
+                remote(
+                    mids[p].at[lax.rem(place[axis] + shift, 4)], got2[p].at[shift - 1],
+                    send.at[p, 1, shift - 1], recv.at[p, 1, shift - 1], peer(axis, shift),
+                )
+                for shift in (1, 2, 3)
+            ]
+        )
+    third = []
+    for p in range(3):
+        for copy in second[p]:
+            copy.wait()
+        ends[p][...] = add(mids[p], got2[p], place[ORDERS[p][1]]).astype(BF16)
+        axis = ORDERS[p][2]
+        third.append(
+            [
+                remote(
+                    ends[p].at[lax.rem(place[axis] + shift, 4)], got3[p].at[shift - 1],
+                    send.at[p, 2, shift - 1], recv.at[p, 2, shift - 1], peer(axis, shift),
+                )
+                for shift in (1, 2, 3)
+            ]
+        )
+    for p in range(3):
+        for copy in third[p]:
+            copy.wait()
+        done[:, PARTS[p] : PARTS[p + 1]] = add(ends[p], got3[p], place[ORDERS[p][2]])
+    keep = pl.ds(pl.multiple_of(core * 8, 8), 8)
+    give = pl.ds(pl.multiple_of((1 - core) * 8, 8), 8)
+    last = remote(done.at[give, :], done_in, core_send.at[3], core_recv.at[3], other)
+    out[:, ours] = done[keep, :]
+    last.wait()
+    out[:, theirs] = done_in[...]
+
+
+def sum_over_devices_call(left, right, small):
+    half = right.shape[1] // 2
+    widths = [PARTS[p + 1] - PARTS[p] for p in range(3)]
+
+    def blocks(*lead):
+        return [pltpu.VMEM(lead + (CORE_ROWS, w), BF16) for w in widths]
+
+    return pl.pallas_call(
+        sum_over_devices,
+        in_specs=[pl.BlockSpec(memory_space=pltpu.VMEM)] * 3,
+        out_specs=[pl.BlockSpec(memory_space=pltpu.VMEM)] * 2,
+        out_shape=(
+            jax.ShapeDtypeStruct((8, 2 * half), F32),
+            jax.ShapeDtypeStruct(small.shape, F32),
+        ),
+        scratch_shapes=[
+            pltpu.VMEM(left.shape, BF16),
+            pltpu.VMEM((left.shape[0], half), BF16),
+            *blocks(4, 4, 4),
+            *blocks(3, 4, 4),
+            *blocks(4, 4),
+            *blocks(3, 4),
+            *blocks(4),
+            *blocks(3),
+            pltpu.VMEM((CORE_ROWS, half), F32),
+            pltpu.VMEM((8, half), F32),
+            pltpu.VMEM((3, 4) + small.shape, F32),
+            pltpu.VMEM(small.shape, F32),
+            pltpu.SemaphoreType.DMA((4,)),
+            pltpu.SemaphoreType.DMA((4,)),
+            pltpu.SemaphoreType.DMA((3, 3, 3)),
+            pltpu.SemaphoreType.DMA((3, 3, 3)),
+            pltpu.SemaphoreType.DMA((3, 3)),
+            pltpu.SemaphoreType.DMA((3, 3)),
+        ],
+        compiler_params=pltpu.CompilerParams(
+            vmem_limit_bytes=VMEM_LIMIT, collective_id=0, has_side_effects=True
+        ),
+        cost_estimate=pl.CostEstimate(
+            flops=1_200_000_000, bytes_accessed=4_000_000, transcendentals=0
+        ),
+        name="sum_over_devices",
+    )(left, right, small)
+
+
 HM = 24
 GROUPS = 8
 HEADS = 8
@@ -525,20 +716,64 @@
     return lax.dynamic_slice_in_dim(block, half * width, width, 1)
 
 
-def weight_gradient(left, right, core):
+def gather_rows(shard, core):
+    rows = shard.shape[0] // 2
+    mine = lax.dynamic_slice_in_dim(shard, core * rows, rows, 0)
+    place = lax.axis_index("fs")
+    got = jnp.stack(
+        [mine]
+        + [lax.ppermute(mine, "fs", [(i, (i + s) % 4) for i in range(4)]) for s in (1, 2, 3)]
+    )
+    order = jnp.mod(place - jnp.arange(4), 4)
+    ours = jnp.take(got, order, axis=0)
+    return ours, other_core(ours)
+
+
+def gather_all(shard, at):
+    rows = shard.shape[0] // 32
+    return lax.all_gather(
+        lax.dynamic_slice_in_dim(shard, at * rows, rows, 0), TOKEN_AXES, axis=0, tiled=True
+    )
+
+
+def both_cores(left, right, core):
     lefts = jnp.concatenate([left, other_core(left)], axis=0)
     rights = jnp.concatenate(
         [columns_half(right, core), other_core(columns_half(right, 1 - core))], axis=0
     )
-    part = tn(lefts, rights).astype(BF16)
-    for axis in ("fs", "cp", "ux"):
-        part = lax.psum_scatter(part, axis, scatter_dimension=0, tiled=True)
-    rows = part.shape[0] // 2
-    mine = lax.dynamic_slice_in_dim(part, core * rows, rows, 0)
-    theirs = other_core(lax.dynamic_slice_in_dim(part, (1 - core) * rows, rows, 0))
+    return lefts, rights
+
+
+def core_halves(rows, core):
+    r = rows.shape[0] // 2
+    mine = lax.dynamic_slice_in_dim(rows, core * r, r, 0)
+    theirs = other_core(lax.dynamic_slice_in_dim(rows, (1 - core) * r, r, 0))
     return jnp.concatenate(
         [jnp.where(core == 0, mine, theirs), jnp.where(core == 0, theirs, mine)], axis=1
     ).astype(F32)
+
+
+def weight_gradients(pairs, core):
+    blocks = []
+    for left, right in pairs:
+        lefts, rights = both_cores(left, right, core)
+        for at in range(0, rights.shape[1], 512):
+            part = tn(lefts, rights[:, at : at + 512]).astype(BF16)
+            blocks.append(part.reshape(64, part.shape[0] // 64, 512))
+    total = jnp.concatenate(blocks, axis=1)
+    for axis in ("fs", "cp", "ux"):
+        total = lax.psum_scatter(total, axis, scatter_dimension=0, tiled=True)
+    total = total[0]
+    results, at = [], 0
+    for left, right in pairs:
+        r = left.shape[1] // 64
+        count = right.shape[1] // 1024
+        whole = jnp.concatenate(
+            [total[at + i * r : at + (i + 1) * r] for i in range(count)], axis=1
+        )
+        at += count * r
+        results.append(core_halves(whole, core))
+    return results
 
 
 def shards(
@@ -563,9 +798,30 @@
     rows = tokens.shape[0]
     length = GROUPS * rows
     heads = HM // GROUPS
-    full_in, full_mout, full_aout, full_gu, full_down = (
-        lax.all_gather(w, "fs", axis=0, tiled=True) for w in (w_in, w_mout, w_aout, w_gu, w_down)
-    )
+    at = part_rank * GROUPS + group
+    in_ours, in_theirs = gather_rows(w_in, core)
+    gu_ours, gu_theirs = gather_rows(w_gu, core)
+    full_mout, full_aout, full_down = (gather_all(w, at) for w in (w_mout, w_aout, w_down))
+
+    def halves(block):
+        pieces = block.reshape(rows, 4, 2, block.shape[1] // 8)
+        picked = [
+            lax.dynamic_index_in_dim(pieces, which, 2, False).reshape(rows, block.shape[1] // 2)
+            for which in (core, 1 - core)
+        ]
+        return picked
+
+    def times_halves(block, ours, theirs):
+        own, rest = halves(block)
+        width = ours.shape[-1]
+        return nn(own, ours.reshape(-1, width)) + nn(rest, theirs.reshape(-1, width))
+
+    def times_halves_transposed(block, ours, theirs):
+        width = ours.shape[-1]
+        own = nt(block, ours.reshape(-1, width)).reshape(rows, 4, -1)
+        rest = nt(block, theirs.reshape(-1, width)).reshape(rows, 4, -1)
+        pieces = jnp.where(core == 0, jnp.stack([own, rest], 2), jnp.stack([rest, own], 2))
+        return pieces.reshape(rows, -1)
 
     def to_groups(blocks):
         return lax.all_to_all(blocks, ("ux", "uc"), split_axis=0, concat_axis=0, tiled=True)
@@ -573,7 +829,7 @@
     resid_in = tokens.astype(F32)
     normed_f, in_back = jax.vjp(rms_norm, resid_in, norm_in)
     normed_in = normed_f.astype(BF16)
-    projected = nn(normed_in, full_in)
+    projected = times_halves(normed_in, in_ours, in_theirs)
     gate_pre = projected[:, :DS]
     low = projected[:, DS:].astype(BF16)
     q_at = DS + 2 * NS + HM
@@ -624,7 +880,7 @@
     resid_mid = resid_in + nn(branch_low, full_mout) + nn(attended_tok, full_aout)
     normed_mid_f, mid_back = jax.vjp(rms_norm, resid_mid, norm_mid)
     normed_mid = normed_mid_f.astype(BF16)
-    gate_up = nn(normed_mid, full_gu)
+    gate_up = times_halves(normed_mid, gu_ours, gu_theirs)
     gate_half = gate_up[:, :FF]
     up_half = gate_up[:, FF:]
     sigmoid_gate = jax.nn.sigmoid(gate_half)
@@ -634,7 +890,9 @@
     grad_gate = grad_hidden * up_half * sigmoid_gate * (1.0 + gate_half * (1.0 - sigmoid_gate))
     grad_up = grad_hidden * gate_half * sigmoid_gate
     grad_gate_up = jnp.concatenate([grad_gate, grad_up], axis=1).astype(BF16)
-    resid_back, grad_norm_mid = mid_back(nt(grad_gate_up, full_gu))
+    resid_back, grad_norm_mid = mid_back(
+        times_halves_transposed(grad_gate_up, gu_ours, gu_theirs)
+    )
     grad_resid = grad_out.astype(F32) + resid_back
     resid_low = grad_resid.astype(BF16)
     grad_mixed, grad_gate_pre, grad_mamba_gain = gate_back(nt(resid_low, full_mout))
@@ -647,10 +905,15 @@
         axis=2,
     ).transpose(1, 0, 2)
     grad = to_groups(grad_blocks).reshape(length, XW + HP)
-    grad_down = weight_gradient(hidden, grad_out, core)
-    grad_gu = weight_gradient(normed_mid, grad_gate_up, core)
-    grad_mout = weight_gradient(branch_low, resid_low, core)
-    grad_aout = weight_gradient(attended_tok, resid_low, core)
+    grad_gu, grad_down, grad_mout, grad_aout = weight_gradients(
+        [
+            (normed_mid, grad_gate_up),
+            (hidden, grad_out),
+            (branch_low, resid_low),
+            (attended_tok, resid_low),
+        ],
+        core,
+    )
 
     entry_gradient = ssd_entry_gradient_call(grad, c_low, cum)
     later = [from_ahead(entry_gradient, d) for d in (1, 2, 3)]
@@ -687,8 +950,9 @@
         ],
         axis=1,
     )
-    grad_in = weight_gradient(normed_in, grad_proj, core)[:, :PROJ]
-    tokens_back, grad_norm_in = in_back(nt(grad_proj[:, :PROJ], full_in))
+    tokens_back, grad_norm_in = in_back(
+        times_halves_transposed(grad_proj[:, :PROJ], in_ours, in_theirs)
+    )
     grad_tokens = grad_resid + tokens_back
 
     conv_full = jnp.concatenate(
@@ -703,9 +967,18 @@
     head_full = lax.dynamic_update_slice_in_dim(
         jnp.zeros((3, HM), F32), grad_par[:3, :heads], group * heads, 1
     )
-    small = lax.psum(
-        (grad_norm_in, grad_norm_mid, grad_mamba_gain, conv_full, head_full), TOKEN_AXES
-    )
+    parts = [
+        a.reshape(-1) for a in (grad_norm_in, grad_norm_mid, grad_mamba_gain, conv_full, head_full)
+    ]
+    flat = jnp.concatenate(parts)
+    flat = jnp.pad(flat, (0, 16 * 1024 - flat.shape[0])).reshape(16, 1024)
+    grad_in, flat = sum_over_devices_call(normed_in, grad_proj, flat)
+    flat = flat.reshape(-1)
+    small, at = [], 0
+    for shape in ((1024,), (1024,), (DS,), (KW, DS + 2 * NS), (3, HM)):
+        size = math.prod(shape)
+        small.append(flat[at : at + size].reshape(shape))
+        at += size
     return (
         layer_out,
         grad_tokens,
@@ -716,7 +989,7 @@
         small[4][0],
         small[4][1],
         small[4][2],
-        grad_in,
+        grad_in[:, :PROJ],
         grad_mout,
         grad_aout,
         grad_gu,

time: 755 us -> 556 us (0.74)
  waiting for transfers between devices: 412 us -> 170 us
  blocking collectives: 81.8 us -> 12.4 us
  Pallas kernels: 50.7 us -> 105 us
  local copies, waits for them, and re-layouts: 47.6 us -> 96.3 us
  other arithmetic: 20 us -> 38.6 us
    reduce_scatter x15 -> x3, waiting for transfers between devices: 165 us -> 36.4 us  [weight_gradients(): total = lax.psum_scatter(total, axis, scatter_dimension=0, tiled=True)]
    all_gather x5 -> x3, waiting for transfers between devices: 184 us -> 58.2 us  [gather_all(): lax.all_gather(lax.dynamic_slice_in_dim(shard, at * rows, rows, 0), TOKEN...]
    psum x1 -> x0, blocking collectives: 66.3 us -> none  [shards(): lax.psum((grad_norm_in, grad_norm_mid, grad_mamba_gain, conv_full, head_f...]
    ppermute x0 -> x6, waiting for transfers between devices: none -> 57.7 us  [gather_rows(): lax.ppermute(mine, 'fs', [(i, (i + s) % 4) for i in range(4)])]
    pallas_call x0 -> x1, Pallas kernels: none -> 54.6 us  [sum_over_devices_call(): pl.pallas_call(sum_over_devices, in_specs=[pl.BlockSpec(memory_space=pltp...]
    all_to_all x3, waiting for transfers between devices: 47.5 us -> 15.7 us  [to_groups(): lax.all_to_all(blocks, ('ux', 'uc'), split_axis=0, concat_axis=0, tiled=T...]
    unnamed x133 -> x146, local copies, waits for them, and re-layouts: 18.4 us -> 31.8 us
    select_n x0 -> x5, local copies, waits for them, and re-layouts: none -> 11.5 us  [the longest x1 6.46 us: gather_rows(): ours = jnp.take(got, order, axis=0)]
  transfers between devices with their start and end apart: 51 -> 42, of which waited for: 24 -> 9; matrix products, arithmetic and copies ran while one was open for 14% -> 33% of each run, Pallas kernels for 7% -> 19%
where the time goes in v2:
time: 556 us; the launch traced here: 545 us
  waiting for transfers between devices  170 us (31%)
  Pallas kernels  105 us (19%)
  local copies, waits for them, and re-layouts  96.3 us (17%)
  starting transfers between devices  54.3 us (10%)
  matrix products  52.9 us (10%)
  other arithmetic  38.6 us (7%)
  between operations  15.7 us (3%)
  blocking collectives  12.4 us (2%)
    all_gather x3, waiting for transfers between devices, gather_all(): lax.all_gather(lax.dynamic_slice_in_dim(shard, at * rows, rows, 0), TOKEN...  58.2 us
    ppermute x6, waiting for transfers between devices, gather_rows(): lax.ppermute(mine, 'fs', [(i, (i + s) % 4) for i in range(4)])  57.7 us
    pallas_call x1, Pallas kernels, sum_over_devices_call(): pl.pallas_call(sum_over_devices, in_specs=[pl.BlockSpec(memory_space=pltp...  54.6 us
    reduce_scatter x3, waiting for transfers between devices, weight_gradients(): total = lax.psum_scatter(total, axis, scatter_dimension=0, tiled=True)  36.4 us
    unnamed x146, local copies, waits for them, and re-layouts  31.8 us
    dot_general x7, matrix products, nt(): lax.dot_general(a, b, (((1,), (1,)), ((), ())), preferred_element_type=F32)  26.1 us
    pallas_call x1, Pallas kernels, ssd_backward_call(): pl.pallas_call(ssd_backward, out_shape=(jax.ShapeDtypeStruct((length, CW)...  22 us
    dot_general x7, matrix products, nn(): lax.dot_general(a, b, (((1,), (0,)), ((), ())), precision=precision, pref...  21.3 us
  transfers between devices with their start and end apart: 42, of which 9 were waited for; matrix products, arithmetic and copies ran while one was open for 33% of the time, Pallas kernels for 19%

profile of v2, /device:TPU:1, one launch (start us, length us, event | category | flops | bytes accessed | tf_op | source)
XLA Modules:
  0.0 545.3 jit_solution(5122466623357542175)
XLA Ops:
  15.2 41.8 %collective-permute-done.2 = bf16[128,4120]{0,1:T(8,128)(2,1)} collective-permute-done((bf16[128,4120]{0,1:T(8,128)(2,1)S(1)}, bf16[128,4120]{0,1:T(8,128)(2,1)}, u32[]{:S(2)}, u32[]{:S(2)}) %collective-permute-start.2) | collective-permute-done | bytes 1054752 | tf_op jit(solution)/shard_map/ppermute | solution.py:725
  57.0 5.1 collective-permute-done
  62.0 3.7 pad_maximum_fusion
  65.7 5.3 gather_fusion
  71.0 4.8 broadcast_select_fusion
  82.1 6.5 %copy.67 = bf16[4,128,4120]{2,1,0:T(8,128)(2,1)} copy(bf16[4,128,4120]{1,2,0:T(8,128)(2,1)} %broadcast_select_fusion) | data formatting | bytes 8437760 | tf_op jit(solution)/shard_map/jit(_take)/select_n | solution.py:728
  91.6 6.5 %copy.69 = bf16[4,128,4120]{2,1,0:T(8,128)(2,1)} copy(bf16[4,128,4120]{1,2,0:T(8,128)(2,1)} %collective-permute-done.3) | data formatting | bytes 8437760 | tf_op jit(solution)/shard_map/ppermute | solution.py:711
  98.1 4.3 fusion.66
  109.6 4.9 all-to-all-start
  117.2 10.9 %collective-permute-done.11 = bf16[128,4096]{1,0:T(8,128)(2,1)} collective-permute-done((bf16[128,4096]{1,0:T(8,128)(2,1)}, bf16[128,4096]{1,0:T(8,128)(2,1)}, u32[]{:S(2)}, u32[]{:S(2)}) %collective-permute-start.11) | collective-permute-done | bytes 1048608 | tf_op jit(solution)/shard_map/ppermute | solution.py:725
  128.1 3.7 pad_maximum_fusion.1
  131.7 5.0 gather_fusion.1
  140.3 4.7 broadcast_select_fusion.1
  155.0 7.4 %ssd_forward.1 = (f32[1024,192]{1,0:T(8,128)}, f32[200,128]{1,0:T(8,128)}, bf16[1024,128]{1,0:T(8,128)(2,1)}, f32[1024,128]{1,0:T(8,128)}, f32[4,192,128]{2,1,0:T(8,128)}) custom-call(bf16[1024,768]{1,0:T(8,128)(2,1)} %bitcast.163, bf16[16,448]{1,0:T(8,128)(2,1)} %copy-done.59, f32[8,448]{1,0:T(8,128)} %select_maximum_fusion.taps, f32[8,128]{1,0:T(8,128)} %pad.13.par), custom_call_target="tpu_custom_call" | custom-call | flops 8000000000 | bytes 8000000 | tf_op jit(solution)/shard_map/ssd_forward/pallas_call | solution.py:121
  167.1 6.1 %attend_forward.1 = (f32[1024,64]{1,0:T(8,128)}, f32[1024,128]{1,0:T(8,128)}) custom-call(s32[1]{0:T(128)} %bitcast.21.rank_ref, bf16[1024,768]{1,0:T(8,128)(2,1)} %bitcast.164, bf16[1024,128]{1,0:T(8,128)(2,1)} %copy-done.53, bf16[1024,128]{1,0:T(8,128)(2,1)} %copy-done.54, bf16[1024,128]{1,0:T(8,128)(2,1)} %copy-done.55), custom_call_target="tpu_custom_call" | custom-call | flops 8000000000 | bytes 4000000 | tf_op jit(solution)/shard_map/attend_forward/pallas_call | solution.py:393
  179.1 7.0 %all-to-all-start.1 = ((bf16[8,128,256]{1,2,0:T(8,128)(2,1)}), bf16[8,128,256]{1,2,0:T(8,128)(2,1)}, u32[]{:S(2)}, u32[]{:S(2)}) async-start(bf16[8,128,256]{1,2,0:T(8,128)(2,1)} %copy.72), calls=%async_computation.1 | async-start | bytes 1048576 | tf_op jit(solution)/shard_map/all_to_all | solution.py:827
  188.2 19.3 %all-gather.8.cloned.1.call-done = bf16[128,12,1024]{2,1,0:T(8,128)(2,1)} async-done(((bf16[1,12,1024]{2,1,0:T(8,128)(2,1)}), bf16[128,12,1024]{2,1,0:T(8,128)(2,1)}) %all-gather.8.cloned.1.call-update) | async-done | bytes 3145744 | tf_op jit(solution)/shard_map/all_gather | solution.py:734
  207.5 4.7 reshape.435
  234.9 4.3 convolution_add_fusion.1
  239.2 38.8 %all-gather.6.cloned.1.call-done = bf16[2048,1024]{1,0:T(8,128)(2,1)} async-done(((bf16[16,1024]{1,0:T(8,128)(2,1)}), bf16[2048,1024]{1,0:T(8,128)(2,1)}) %all-gather.6.cloned.1.call-update) | async-done | bytes 4194320 | tf_op jit(solution)/shard_map/all_gather | solution.py:734
  278.1 5.4 multiply_convert_fusion.1
  283.5 3.8 convolution_bitcast_fusion.4
  326.2 12.4 %all_to_all.20 = bf16[8,128,256]{1,2,0:T(8,128)(2,1)S(1)} all-to-all(bf16[8,128,256]{1,2,0:T(8,128)(2,1)S(1)} %maximum_bitcast_fusion), channel_id=1, replica_groups=mesh['fs'=4,'cp'=4,'ux'=4,'uc'=2] {'ux','uc'}, dimensions={0} | all-to-all | bytes 1048576 | tf_op jit(solution)/shard_map/all_to_all | solution.py:827
  346.2 9.2 %attend_backward.1 = (f32[1024,64]{1,0:T(8,128)}, f32[1024,128]{1,0:T(8,128)}, bf16[1024,128]{1,0:T(8,128)(2,1)}, bf16[1024,128]{1,0:T(8,128)(2,1)}, bf16[1024,128]{1,0:T(8,128)(2,1)}) custom-call(s32[1]{0:T(128)} %bitcast.21.rank_ref, bf16[1024,768]{1,0:T(8,128)(2,1)} %bitcast.165, bf16[1024,128]{1,0:T(8,128)(2,1)} %copy-done.53, ...), custom_call_target="tpu_custom_call" | custom-call | flops 20000000000 | bytes 4000000 | tf_op jit(solution)/shard_map/attend_backward/pallas_call | solution.py:467
  358.0 36.4 %reduce-scatter.4.cloned.1.call-done = bf16[16,128,512]{2,1,0:T(8,128)(2,1)} async-done(((bf16[64,128,512]{2,1,0:T(8,128)(2,1)}), bf16[16,128,512]{2,1,0:T(8,128)(2,1)}) %reduce-scatter.4.cloned.1.call-update) | async-done | bytes 2097168 | tf_op jit(solution)/shard_map/reduce_scatter | solution.py:765
  396.8 22.0 %ssd_backward.1 = (f32[1024,448]{1,0:T(8,128)}, f32[1024,128]{1,0:T(8,128)}, f32[8,448]{1,0:T(8,128)}, f32[8,448]{1,0:T(8,128)}, f32[8,128]{1,0:T(8,128)}) custom-call(bf16[1024,768]{1,0:T(8,128)(2,1)} %bitcast.166, bf16[16,448]{1,0:T(8,128)(2,1)} %copy-done.59, f32[8,448]{1,0:T(8,128)} %select_maximum_fusion.taps, f32[8,128]{1,0:T(8,128)} %pad.13.par, ...), custom_call_target="tpu_custom_call" | custom-call | flops 20000000000 | bytes 12000000 | tf_op jit(solution)/shard_map/ssd_backward/pallas_call | solution.py:314
  427.5 5.6 %all-to-all-start.3 = ((bf16[8,128,768]{1,2,0:T(8,128)(2,1)}), bf16[8,128,768]{1,2,0:T(8,128)(2,1)S(1)}, u32[]{:S(2)}, u32[]{:S(2)}) async-start(bf16[8,128,768]{1,2,0:T(8,128)(2,1)} %copy.82), calls=%async_computation.3 | async-start | bytes 3145728 | tf_op jit(solution)/shard_map/all_to_all | solution.py:827
  433.2 3.7 fusion.2
  438.2 15.7 %all-to-all-done.3 = bf16[8,128,768]{1,2,0:T(8,128)(2,1)S(1)} async-done(((bf16[8,128,768]{1,2,0:T(8,128)(2,1)}), bf16[8,128,768]{1,2,0:T(8,128)(2,1)S(1)}, u32[]{:S(2)}, u32[]{:S(2)}) %all-to-all-start.3) | async-done | bytes 1572896 | tf_op jit(solution)/shard_map/all_to_all | solution.py:827
  455.8 4.0 convolution_bitcast_fusion.2
  459.8 4.0 convolution_bitcast_fusion.1
  468.2 54.6 %sum_over_devices.1 = (f32[8,4352]{1,0:T(8,128)}, f32[16,1024]{1,0:T(8,128)}) custom-call(bf16[128,1024]{1,0:T(8,128)(2,1)} %copy-done.15, bf16[128,4352]{1,0:T(8,128)(2,1)} %concatenate.107.right, f32[16,1024]{1,0:T(8,128)} %reshape.407.small), custom_call_target="tpu_custom_call" | custom-call | flops 1200000000 | bytes 4000000 | tf_op jit(solution)/shard_map/sum_over_devices/pallas_call | solution.py:642
  (369 shorter events, 158.4 us)
Async XLA Ops:
  7.2 178.9 %all-gather.10.cloned.1.call-start = ((), (), s32[]{:S(2)}) async-start(), calls=%async_computation.12 | async-start | bytes 1056768 | tf_op jit(solution)/shard_map/all_gather | solution.py:734
  8.7 198.8 %all-gather.8.cloned.1.call-start = ((), (), s32[]{:S(2)}) async-start(), calls=%async_computation.11 | async-start | bytes 4227072 | tf_op jit(solution)/shard_map/all_gather | solution.py:734
  8.9 48.1 %collective-permute-start.2 = (bf16[128,4120]{0,1:T(8,128)(2,1)S(1)}, bf16[128,4120]{0,1:T(8,128)(2,1)}, u32[]{:S(2)}, u32[]{:S(2)}) collective-permute-start(bf16[128,4120]{0,1:T(8,128)(2,1)S(1)} %constant_dynamic-slice_fusion.14), channel_id=1, source_target_pairs={{0,96},{32,0},{64,32},{96,64},{1,97},{33,1},{65,33},{97,65},{2,98}... | collective-permute-start | bytes 3164168 | tf_op jit(solution)/shard_map/ppermute | solution.py:725
  12.5 44.5 %collective-permute-start.1 = (bf16[128,4120]{0,1:T(8,128)(2,1)S(1)}, bf16[128,4120]{0,1:T(8,128)(2,1)}, u32[]{:S(2)}, u32[]{:S(2)}) collective-permute-start(bf16[128,4120]{0,1:T(8,128)(2,1)S(1)} %constant_dynamic-slice_fusion.14), channel_id=1, source_target_pairs={{0,64},{32,96},{64,0},{96,32},{1,65},{33,97},{65,1},{97,33},{2,66}... | collective-permute-start | bytes 3164168 | tf_op jit(solution)/shard_map/ppermute | solution.py:725
  12.9 49.2 %collective-permute-start = (bf16[128,4120]{0,1:T(8,128)(2,1)S(1)}, bf16[128,4120]{0,1:T(8,128)(2,1)}, u32[]{:S(2)}, u32[]{:S(2)}) collective-permute-start(bf16[128,4120]{0,1:T(8,128)(2,1)S(1)} %constant_dynamic-slice_fusion.14), channel_id=1, source_target_pairs={{0,32},{32,64},{64,96},{96,0},{1,33},{33,65},{65,97},{97,1},{2,34}... | collective-permute-start | bytes 3164168 | tf_op jit(solution)/shard_map/ppermute | solution.py:725
  15.0 263.1 %all-gather.6.cloned.1.call-start = ((), (), s32[]{:S(2)}) async-start(), calls=%async_computation.7 | async-start | bytes 4227072 | tf_op jit(solution)/shard_map/all_gather | solution.py:734
  75.7 15.9 %collective-permute-start.3 = (bf16[4,128,4120]{1,2,0:T(8,128)(2,1)}, bf16[4,128,4120]{1,2,0:T(8,128)(2,1)}, u32[]{:S(2)}, u32[]{:S(2)}) collective-permute-start(bf16[4,128,4120]{1,2,0:T(8,128)(2,1)} %broadcast_select_fusion), channel_id=1, source_target_pairs={{0,1},{1,0},{2,3},{3,2},{4,5},{5,4},{6,7},{7,6},{8,9},{9,8},{10,11... | collective-permute-start | bytes 12656648 | tf_op jit(solution)/shard_map/ppermute | solution.py:711
  77.3 39.9 %collective-permute-start.13 = (bf16[128,4096]{1,0:T(8,128)(2,1)}, bf16[128,4096]{1,0:T(8,128)(2,1)}, u32[]{:S(2)}, u32[]{:S(2)}) collective-permute-start(bf16[128,4096]{1,0:T(8,128)(2,1)} %constant_dynamic-slice_fusion.9), channel_id=1, source_target_pairs={{0,96},{32,0},{64,32},{96,64},{1,97},{33,1},{65,33},{97,65},{2,98}... | collective-permute-start | bytes 3145736 | tf_op jit(solution)/shard_map/ppermute | solution.py:725
  77.6 39.5 %collective-permute-start.12 = (bf16[128,4096]{1,0:T(8,128)(2,1)}, bf16[128,4096]{1,0:T(8,128)(2,1)}, u32[]{:S(2)}, u32[]{:S(2)}) collective-permute-start(bf16[128,4096]{1,0:T(8,128)(2,1)} %constant_dynamic-slice_fusion.9), channel_id=1, source_target_pairs={{0,64},{32,96},{64,0},{96,32},{1,65},{33,97},{65,1},{97,33},{2,66}... | collective-permute-start | bytes 3145736 | tf_op jit(solution)/shard_map/ppermute | solution.py:725
  78.0 50.1 %collective-permute-start.11 = (bf16[128,4096]{1,0:T(8,128)(2,1)}, bf16[128,4096]{1,0:T(8,128)(2,1)}, u32[]{:S(2)}, u32[]{:S(2)}) collective-permute-start(bf16[128,4096]{1,0:T(8,128)(2,1)} %constant_dynamic-slice_fusion.9), channel_id=1, source_target_pairs={{0,32},{32,64},{64,96},{96,0},{1,33},{33,65},{65,97},{97,1},{2,34}... | collective-permute-start | bytes 3145736 | tf_op jit(solution)/shard_map/ppermute | solution.py:725
  109.6 27.2 %all-to-all-start = ((bf16[8,128,768]{2,1,0:T(8,128)(2,1)}), bf16[8,128,768]{2,1,0:T(8,128)(2,1)S(1)}, u32[]{:S(2)}, u32[]{:S(2)}) async-start(bf16[8,128,768]{2,1,0:T(8,128)(2,1)} %bitcast_dynamic-update-slice_fusion), calls=%async_computation | async-start | bytes 3145728 | tf_op jit(solution)/shard_map/all_to_all | solution.py:827
  136.7 17.7 %collective-permute-start.4 = (bf16[16,448]{1,0:T(8,128)(2,1)S(1)}, bf16[16,448]{1,0:T(8,128)(2,1)S(1)}, u32[]{:S(2)}, u32[]{:S(2)}) collective-permute-start(bf16[16,448]{1,0:T(8,128)(2,1)S(1)} %slice.384), channel_id=1, source_target_pairs={{0,8},{8,16},{16,24},{1,9},{9,17},{17,25},{2,10},{10,18},{18,26},{... | collective-permute-start | bytes 43016 | tf_op jit(solution)/shard_map/ppermute | solution.py:703
  144.9 90.0 %collective-permute-start.14 = (bf16[4,128,4096]{2,1,0:T(8,128)(2,1)}, bf16[4,128,4096]{2,1,0:T(8,128)(2,1)}, u32[]{:S(2)}, u32[]{:S(2)}) collective-permute-start(bf16[4,128,4096]{2,1,0:T(8,128)(2,1)} %broadcast_select_fusion.1), channel_id=1, source_target_pairs={{0,1},{1,0},{2,3},{3,2},{4,5},{5,4},{6,7},{7,6},{8,9},{9,8},{10,11... | collective-permute-start | bytes 12582920 | tf_op jit(solution)/shard_map/ppermute | solution.py:711
  145.7 18.0 %collective-permute-start.8 = (bf16[1024,128]{1,0:T(8,128)(2,1)S(1)}, bf16[1024,128]{1,0:T(8,128)(2,1)S(1)}, u32[]{:S(2)}, u32[]{:S(2)}) collective-permute-start(bf16[1024,128]{1,0:T(8,128)(2,1)S(1)} %slice.385), channel_id=1, source_target_pairs={{0,8},{8,16},{16,24},{1,9},{9,17},{17,25},{2,10},{10,18},{18,26},{... | collective-permute-start | bytes 786440 | tf_op jit(solution)/shard_map/ppermute | solution.py:703
  149.3 15.7 %collective-permute-start.9 = (bf16[1024,128]{1,0:T(8,128)(2,1)S(1)}, bf16[1024,128]{1,0:T(8,128)(2,1)S(1)}, u32[]{:S(2)}, u32[]{:S(2)}) collective-permute-start(bf16[1024,128]{1,0:T(8,128)(2,1)S(1)} %slice.385), channel_id=1, source_target_pairs={{0,16},{8,24},{1,17},{9,25},{2,18},{10,26},{3,19},{11,27},{4,20},{... | collective-permute-start | bytes 786440 | tf_op jit(solution)/shard_map/ppermute | solution.py:703
  152.9 13.5 %collective-permute-start.10 = (bf16[1024,128]{1,0:T(8,128)(2,1)S(1)}, bf16[1024,128]{1,0:T(8,128)(2,1)S(1)}, u32[]{:S(2)}, u32[]{:S(2)}) collective-permute-start(bf16[1024,128]{1,0:T(8,128)(2,1)S(1)} %slice.385), channel_id=1, source_target_pairs={{0,24},{1,25},{2,26},{3,27},{4,28},{5,29},{6,30},{7,31},{32,56},{3... | collective-permute-start | bytes 786440 | tf_op jit(solution)/shard_map/ppermute | solution.py:703
  162.4 10.7 %collective-permute-start.5 = (f32[200,128]{1,0:T(8,128)}, f32[200,128]{1,0:T(8,128)S(1)}, u32[]{:S(2)}, u32[]{:S(2)}) collective-permute-start(f32[200,128]{1,0:T(8,128)} %get-tuple-element.38), channel_id=1, source_target_pairs={{0,8},{8,16},{16,24},{1,9},{9,17},{17,25},{2,10},{10,18},{18,26},{... | collective-permute-start | bytes 307208 | tf_op jit(solution)/shard_map/ppermute | solution.py:703
  163.7 9.4 %collective-permute-start.6 = (f32[200,128]{1,0:T(8,128)}, f32[200,128]{1,0:T(8,128)S(1)}, u32[]{:S(2)}, u32[]{:S(2)}) collective-permute-start(f32[200,128]{1,0:T(8,128)} %get-tuple-element.38), channel_id=1, source_target_pairs={{0,16},{8,24},{1,17},{9,25},{2,18},{10,26},{3,19},{11,27},{4,20},{... | collective-permute-start | bytes 307208 | tf_op jit(solution)/shard_map/ppermute | solution.py:703
  179.1 33.2 %all-to-all-start.1 = ((bf16[8,128,256]{1,2,0:T(8,128)(2,1)}), bf16[8,128,256]{1,2,0:T(8,128)(2,1)}, u32[]{:S(2)}, u32[]{:S(2)}) async-start(bf16[8,128,256]{1,2,0:T(8,128)(2,1)} %copy.72), calls=%async_computation.1 | async-start | bytes 1048576 | tf_op jit(solution)/shard_map/all_to_all | solution.py:827
  186.0 208.4 %reduce-scatter.4.cloned.1.call-start = ((), (), s32[]{:S(2)}) async-start(), calls=%async_computation.8 | async-start | bytes 10485760 | tf_op jit(solution)/shard_map/reduce_scatter | solution.py:765
  220.7 82.1 %collective-permute-start.26 = (bf16[128,1536]{1,0:T(8,128)(2,1)}, bf16[128,1536]{1,0:T(8,128)(2,1)}, u32[]{:S(2)}, u32[]{:S(2)}) collective-permute-start(bf16[128,1536]{1,0:T(8,128)(2,1)} %multiply_convert_fusion.4), channel_id=1, source_target_pairs={{0,1},{1,0},{2,3},{3,2},{4,5},{5,4},{6,7},{7,6},{8,9},{9,8},{10,11... | collective-permute-start | bytes 1179656 | tf_op jit(solution)/shard_map/ppermute | solution.py:711
  302.5 9.2 %collective-permute-start.25 = (bf16[128,512]{1,0:T(8,128)(2,1)S(1)}, bf16[128,512]{1,0:T(8,128)(2,1)S(1)}, u32[]{:S(2)}, u32[]{:S(2)}) collective-permute-start(bf16[128,512]{1,0:T(8,128)(2,1)S(1)} %get-tuple-element.102), channel_id=1, source_target_pairs={{0,1},{1,0},{2,3},{3,2},{4,5},{5,4},{6,7},{7,6},{8,9},{9,8},{10,11... | collective-permute-start | bytes 393224 | tf_op jit(solution)/shard_map/ppermute | solution.py:711
  302.8 12.6 %collective-permute-start.28 = (bf16[128,512]{0,1:T(8,128)(2,1)S(1)}, bf16[128,512]{0,1:T(8,128)(2,1)S(1)}, u32[]{:S(2)}, u32[]{:S(2)}) collective-permute-start(bf16[128,512]{0,1:T(8,128)(2,1)S(1)} %bitcast.180), channel_id=1, source_target_pairs={{0,1},{1,0},{2,3},{3,2},{4,5},{5,4},{6,7},{7,6},{8,9},{9,8},{10,11... | collective-permute-start | bytes 393224 | tf_op jit(solution)/shard_map/ppermute | solution.py:711
  316.6 151.6 %reduce-scatter.6.cloned.1.call-start = ((), (), s32[]{:S(2)}) async-start(), calls=%async_computation.9 | async-start | bytes 2621440 | tf_op jit(solution)/shard_map/reduce_scatter | solution.py:765
  342.3 52.1 %collective-permute-start.15 = (f32[200,128]{1,0:T(8,128)}, f32[200,128]{1,0:T(8,128)S(1)}, u32[]{:S(2)}, u32[]{:S(2)}) collective-permute-start(f32[200,128]{1,0:T(8,128)} %ssd_entry_gradient.1), channel_id=1, source_target_pairs={{8,0},{16,8},{24,16},{9,1},{17,9},{25,17},{10,2},{18,10},{26,18},{... | collective-permute-start | bytes 307208 | tf_op jit(solution)/shard_map/ppermute | solution.py:707
  343.6 52.5 %collective-permute-start.16 = (f32[200,128]{1,0:T(8,128)}, f32[200,128]{1,0:T(8,128)S(1)}, u32[]{:S(2)}, u32[]{:S(2)}) collective-permute-start(f32[200,128]{1,0:T(8,128)} %ssd_entry_gradient.1), channel_id=1, source_target_pairs={{16,0},{24,8},{17,1},{25,9},{18,2},{26,10},{19,3},{27,11},{20,4},{... | collective-permute-start | bytes 307208 | tf_op jit(solution)/shard_map/ppermute | solution.py:707
  344.9 51.2 %collective-permute-start.17 = (f32[200,128]{1,0:T(8,128)}, f32[200,128]{1,0:T(8,128)S(1)}, u32[]{:S(2)}, u32[]{:S(2)}) collective-permute-start(f32[200,128]{1,0:T(8,128)} %ssd_entry_gradient.1), channel_id=1, source_target_pairs={{24,0},{25,1},{26,2},{27,3},{28,4},{29,5},{30,6},{31,7},{56,32},{5... | collective-permute-start | bytes 307208 | tf_op jit(solution)/shard_map/ppermute | solution.py:707
  355.4 70.0 %collective-permute-start.21 = (bf16[1024,128]{1,0:T(8,128)(2,1)}, bf16[1024,128]{1,0:T(8,128)(2,1)S(1)}, u32[]{:S(2)}, u32[]{:S(2)}) collective-permute-start(bf16[1024,128]{1,0:T(8,128)(2,1)} %get-tuple-element.50), channel_id=1, source_target_pairs={{24,0},{25,1},{26,2},{27,3},{28,4},{29,5},{30,6},{31,7},{56,32},{5... | collective-permute-start | bytes 786440 | tf_op jit(solution)/shard_map/ppermute | solution.py:707
  356.7 68.7 %collective-permute-start.20 = (bf16[1024,128]{1,0:T(8,128)(2,1)}, bf16[1024,128]{1,0:T(8,128)(2,1)S(1)}, u32[]{:S(2)}, u32[]{:S(2)}) collective-permute-start(bf16[1024,128]{1,0:T(8,128)(2,1)} %get-tuple-element.49), channel_id=1, source_target_pairs={{16,0},{24,8},{17,1},{25,9},{18,2},{26,10},{19,3},{27,11},{20,4},{... | collective-permute-start | bytes 786440 | tf_op jit(solution)/shard_map/ppermute | solution.py:707
  394.4 31.0 %collective-permute-start.19 = (bf16[1024,128]{1,0:T(8,128)(2,1)}, bf16[1024,128]{1,0:T(8,128)(2,1)S(1)}, u32[]{:S(2)}, u32[]{:S(2)}) collective-permute-start(bf16[1024,128]{1,0:T(8,128)(2,1)} %get-tuple-element.48), channel_id=1, source_target_pairs={{8,0},{16,8},{24,16},{9,1},{17,9},{25,17},{10,2},{18,10},{26,18},{... | collective-permute-start | bytes 786440 | tf_op jit(solution)/shard_map/ppermute | solution.py:707
  427.5 26.3 %all-to-all-start.3 = ((bf16[8,128,768]{1,2,0:T(8,128)(2,1)}), bf16[8,128,768]{1,2,0:T(8,128)(2,1)S(1)}, u32[]{:S(2)}, u32[]{:S(2)}) async-start(bf16[8,128,768]{1,2,0:T(8,128)(2,1)} %copy.82), calls=%async_computation.3 | async-start | bytes 3145728 | tf_op jit(solution)/shard_map/all_to_all | solution.py:827
  433.1 98.3 %reduce-scatter.8.cloned.1.call-start = ((), (), s32[]{:S(2)}) async-start(), calls=%async_computation.10 | async-start | bytes 655360 | tf_op jit(solution)/shard_map/reduce_scatter | solution.py:765
  (71 other events, 576.3 us)
Sparse Core Ops, SparseCore 0:
  11.4 118.6 all-gather.9
  133.8 73.6 all-gather.7
  211.2 66.8 all-gather.5
  316.7 77.6 reduce-scatter.3
  396.6 29.6 reduce-scatter.5
  468.3 30.0 reduce-scatter.7
